TPU v7x, 128 devices: a whole 4x4x4 slice. The times are simulated.
128 devices in a mesh: dp: 8 (over y_hi, x), head: 8 (over z, core), pair: 2 (over y_lo).
Axes of the slice: x: 4, y: 4 (y_hi: 2, y_lo: 2; y = y_hi * 2 + y_lo), z: 4, core: 2. Of those that a mesh axis runs over, the one named last changes fastest.
Arguments:
- hidden: bfloat16 [8, 2, 384, 4096], P('dp', 'pair'), may hold values from -200 to 200
- d_out: bfloat16 [8, 2, 384, 4096], P('dp', 'pair'), may hold values from -0.59765625 to 0.59765625
- norm_gain: float32 [4096], replicated, may hold values from 0.1 to 1.9
- w_query: bfloat16 [4096, 4096], P(('dp', 'pair'), 'head'), may hold values from -1 to 1
- w_key: bfloat16 [4096, 1024], P(('dp', 'pair'), 'head'), may hold values from -1 to 1
- w_value: bfloat16 [4096, 1024], P(('dp', 'pair'), 'head'), may hold values from -0.25 to 0.25
- w_out: bfloat16 [4096, 4096], P('head', ('dp', 'pair')), may hold values from -0.5 to 0.5
- prompt_len: int32 [8], P('dp'), may hold values from 257 to 512, as said below
- resp_len: int32 [8, 2], P('dp', 'pair'), may hold values from 32 to 128, as said below
Outputs:
- branch: bfloat16 [8, 2, 384, 4096], P('dp', 'pair', None, 'head')
- grad_hidden: float32 [8, 2, 384, 4096], P('dp', 'pair', None, 'head')
- grad_w_query: float32 [4096, 4096], P(('dp', 'pair'), 'head')
- grad_w_key: float32 [4096, 1024], P(('dp', 'pair'), 'head')
- grad_w_value: float32 [4096, 1024], P(('dp', 'pair'), 'head')
- grad_w_out: float32 [4096, 4096], P('head', ('dp', 'pair'))
- grad_gain: float32 [4096], replicated
Inputs may be any that keep to these rules, and one draw needn't show every extreme that they name: The live prompt of pair b is prompt slots 0 to prompt_len[b] - 1 of its 512; in every draw some pair's prompt fills all of them. The live response tokens are the first resp_len slots of that response; in every draw some response fills all 128.
All inputs are finite; a program needn't handle non-finite values.
Results may differ from a plain program's by a relative error of at most 0.02.
The roundings to bfloat16 on the way count: a program that leaves them out, or rounds other values in their place, can miss the bound.
Values may be sent and summed in bfloat16 or wider, within the bound.
A program may use at most 128 MiB of HBM per device.

v0:
```python
import jax
import jax.numpy as jnp
from jax import lax
from jax.sharding import PartitionSpec as P

HEAD_DIM = 128
HALF = 256
RESP = 128


EPS = 1e-05
BASE = 500000.0


def swapped(block, axis, bit):
    count = lax.axis_size(axis)
    route = []
    for low in range(count):
        high = low | 1 << bit
        if high != low and high < count:
            route += [(low, high), (high, low)]
    return lax.ppermute(block, axis, route)


def rope_tables(positions):
    half_dim = HEAD_DIM // 2
    steps = jnp.arange(half_dim, dtype=jnp.float32) * (2.0 / HEAD_DIM)
    freqs = jnp.exp(-steps * jnp.log(jnp.float32(BASE)))
    angles = positions.astype(jnp.float32)[..., None] * freqs
    return (jnp.cos(angles), jnp.sin(angles))


def rotate(values, cosine, sine):
    first = values[..., : HEAD_DIM // 2]
    second = values[..., HEAD_DIM // 2 :]
    return jnp.concatenate([first * cosine - second * sine, second * cosine + first * sine], -1)


def unrotate(grads, cosine, sine):
    first = grads[..., : HEAD_DIM // 2]
    second = grads[..., HEAD_DIM // 2 :]
    return jnp.concatenate([first * cosine + second * sine, second * cosine - first * sine], -1)


def positions_of(partner, prompt_length):
    slot_ids = jnp.arange(HALF + RESP, dtype=jnp.int32)
    return jnp.where(slot_ids < HALF, partner * HALF + slot_ids, prompt_length + slot_ids - HALF)


def allowed(q_partner, q_slot, k_partner, k_slot, prompt_length, resp_length):
    q_prompt = q_slot < HALF
    k_prompt = k_slot < HALF
    q_place = q_partner * HALF + q_slot
    k_place = k_partner * HALF + k_slot
    prompt_key = k_prompt & (k_place < prompt_length) & (~q_prompt | (k_place <= q_place))
    resp_key = (
        ~k_prompt
        & ~q_prompt
        & (k_partner == q_partner)
        & (k_slot <= q_slot)
        & (k_slot - HALF < resp_length)
    )
    return prompt_key | resp_key


def attend_head(query, keys, values, mask):
    scores = jnp.einsum(
        "sgd,td->gst", query, keys, preferred_element_type=jnp.float32
    ) * HEAD_DIM ** (-0.5)
    scores = jnp.where(mask, scores, -jnp.inf)
    row_max = jnp.max(scores, -1, keepdims=True)
    expo = jnp.exp(scores - row_max)
    probs = expo / jnp.sum(expo, -1, keepdims=True)
    rounded = probs.astype(jnp.bfloat16)
    attended = jnp.einsum("gst,td->sgd", rounded, values, preferred_element_type=jnp.float32)
    return (probs, rounded, attended)


def contract_last(left, right):
    return lax.dot_general(
        left, right, (((1,), (1,)), ((), ())), preferred_element_type=jnp.float32
    )


def contract_first(left, right):
    return lax.dot_general(
        left, right, (((0,), (0,)), ((), ())), preferred_element_type=jnp.float32
    )


def shards(hidden, d_out, norm_gain, w_query, w_key, w_value, w_out, prompt_len, resp_len):
    inputs = hidden[0, 0].astype(jnp.float32)
    slots_all, width = inputs.shape
    inverse_rms = lax.rsqrt(jnp.mean(inputs * inputs, -1, keepdims=True) + EPS)
    scaled_in = inputs * inverse_rms
    normed = (scaled_in * norm_gain).astype(jnp.bfloat16)
    partner = lax.axis_index("pair")
    prompt_length = prompt_len[0]
    resp_length = resp_len[0, 0]
    cosine, sine = rope_tables(positions_of(partner, prompt_length))
    cosine = cosine[:, None, :]
    sine = sine[:, None, :]
    q_cols = w_query.shape[1]
    kv_cols = w_key.shape[1]
    heads_dev = q_cols // HEAD_DIM
    kv_dev = kv_cols // HEAD_DIM
    group = heads_dev // kv_dev
    w_local = jnp.concatenate([w_query, w_key, w_value], 1)
    part = normed
    projected = jnp.dot(
        part,
        lax.all_gather(w_local, ("dp", "pair"), axis=0, tiled=True),
        preferred_element_type=jnp.float32,
    )
    query = rotate(
        projected[:, :q_cols].reshape(slots_all, heads_dev, HEAD_DIM), cosine, sine
    ).astype(jnp.bfloat16)
    keys = rotate(
        projected[:, q_cols : q_cols + kv_cols].reshape(slots_all, kv_dev, HEAD_DIM), cosine, sine
    )
    keys = keys.astype(jnp.bfloat16).reshape(slots_all, kv_cols)
    values = projected[:, q_cols + kv_cols :].astype(jnp.bfloat16)
    pages = jnp.stack([keys[:HALF], values[:HALF]])
    other = swapped(pages, "pair", 0)
    leading = partner == 0
    first = jnp.where(leading, pages, other)
    second = jnp.where(leading, other, pages)
    keys_all = jnp.concatenate([first[0], second[0], keys[HALF:]])
    values_all = jnp.concatenate([first[1], second[1], values[HALF:]])
    slot_ids = jnp.arange(slots_all, dtype=jnp.int32)
    half_ids = jnp.arange(HALF, dtype=jnp.int32)
    key_partner = jnp.concatenate(
        [
            jnp.zeros((HALF,), jnp.int32),
            jnp.ones((HALF,), jnp.int32),
            jnp.zeros((slots_all - HALF,), jnp.int32) + partner,
        ]
    )
    key_slot = jnp.concatenate([half_ids, half_ids, slot_ids[HALF:]])
    mask = allowed(
        partner,
        slot_ids[:, None],
        key_partner[None, :],
        key_slot[None, :],
        prompt_length,
        resp_length,
    )
    q_head = query
    k_head = keys_all
    v_head = values_all
    probs, rounded, attended_f = attend_head(q_head, k_head, v_head, mask)
    saved = (q_head, k_head, v_head, probs, rounded, attended_f)
    pieces = attended_f.astype(jnp.bfloat16).reshape(slots_all, group * HEAD_DIM)
    partial_out = jnp.dot(
        pieces,
        lax.all_gather(w_out, ("dp", "pair"), axis=1, tiled=True),
        preferred_element_type=jnp.float32,
    )
    branch = lax.psum_scatter(
        partial_out.astype(jnp.bfloat16), "head", scatter_dimension=1, tiled=True
    )
    cotangent = d_out[0, 0]
    part = cotangent
    grad_attended = contract_last(part, lax.all_gather(w_out, ("dp", "pair"), axis=1, tiled=True))
    grad_attended = grad_attended.astype(jnp.bfloat16)
    part = cotangent
    grad_w_out = (
        lax.psum_scatter(
            contract_first(part, pieces).astype(jnp.bfloat16),
            ("dp", "pair"),
            scatter_dimension=0,
            tiled=True,
        )
        .astype(jnp.float32)
        .T
    )
    q_head, k_head, v_head, probs, rounded, attended_f = saved
    g_head = grad_attended
    g_head = g_head.reshape(slots_all, group, HEAD_DIM)
    d_probs = jnp.einsum("sgd,td->gst", g_head, v_head, preferred_element_type=jnp.float32)
    delta = jnp.sum(g_head.astype(jnp.float32) * attended_f, -1).T[:, :, None]
    d_scores = (probs * (d_probs - delta) * HEAD_DIM ** (-0.5)).astype(jnp.bfloat16)
    d_queries = jnp.einsum("gst,td->sgd", d_scores, k_head, preferred_element_type=jnp.float32)
    d_keys = jnp.einsum("gst,sgd->td", d_scores, q_head, preferred_element_type=jnp.float32)
    d_values = jnp.einsum("gst,sgd->td", rounded, g_head, preferred_element_type=jnp.float32)
    key_grads = jnp.stack([d_keys, d_values])
    lower = key_grads[:, :HALF]
    upper = key_grads[:, HALF : 2 * HALF]
    mine = jnp.where(leading, lower, upper)
    theirs = jnp.where(leading, upper, lower)
    returned = swapped(theirs.astype(jnp.bfloat16), "pair", 0).astype(theirs.dtype)
    prompt_grads = mine + returned
    d_key_rows = jnp.concatenate([prompt_grads[0], key_grads[0, 2 * HALF :]])
    d_value_rows = jnp.concatenate([prompt_grads[1], key_grads[1, 2 * HALF :]])
    d_query_b = unrotate(d_queries, cosine, sine).astype(jnp.bfloat16).reshape(slots_all, q_cols)
    d_key_b = unrotate(d_key_rows.reshape(slots_all, kv_dev, HEAD_DIM), cosine, sine)
    d_key_b = d_key_b.astype(jnp.bfloat16).reshape(slots_all, kv_cols)
    d_proj = jnp.concatenate([d_query_b, d_key_b, d_value_rows.astype(jnp.bfloat16)], 1)
    part = normed
    grad_local = lax.psum_scatter(
        contract_first(part, d_proj).astype(jnp.bfloat16),
        ("dp", "pair"),
        scatter_dimension=0,
        tiled=True,
    ).astype(jnp.float32)
    d_norm = contract_last(d_proj, lax.all_gather(w_local, ("dp", "pair"), axis=0, tiled=True))
    d_share = lax.psum_scatter(
        d_norm.astype(jnp.bfloat16), "head", scatter_dimension=1, tiled=True
    ).astype(jnp.float32)
    cols = d_share.shape[1]
    offset = lax.axis_index("head") * cols
    scaled_share = lax.dynamic_slice_in_dim(scaled_in, offset, cols, 1)
    gain_share = lax.dynamic_slice_in_dim(norm_gain, offset, cols, 0)
    d_scaled = d_share * gain_share
    row_part = jnp.sum(d_scaled * scaled_share, -1)
    gain_part = jnp.sum(d_share * scaled_share, 0)
    row_total = lax.psum(row_part, "head")
    d_input = inverse_rms * (d_scaled - scaled_share * (row_total / width)[:, None])
    gain_sum = lax.psum(gain_part, ("dp", "pair"))
    grad_gain = lax.all_gather(gain_sum, "head", axis=0, tiled=True)
    return (
        branch[None, None],
        d_input[None, None],
        grad_local[:, :q_cols],
        grad_local[:, q_cols : q_cols + kv_cols],
        grad_local[:, q_cols + kv_cols :],
        grad_w_out,
        grad_gain,
    )


def solution(mesh):
    in_specs = (
        P("dp", "pair", None, None),
        P("dp", "pair", None, None),
        P(),
        P(("dp", "pair"), "head"),
        P(("dp", "pair"), "head"),
        P(("dp", "pair"), "head"),
        P("head", ("dp", "pair")),
        P("dp"),
        P("dp", "pair"),
    )
    out_specs = (
        P("dp", "pair", None, "head"),
        P("dp", "pair", None, "head"),
        P(("dp", "pair"), "head"),
        P(("dp", "pair"), "head"),
        P(("dp", "pair"), "head"),
        P("head", ("dp", "pair")),
        P(),
    )
    return jax.shard_map(shards, mesh=mesh, in_specs=in_specs, out_specs=out_specs, check_vma=False)
```

profile of v0, /device:TPU:1, one launch (start us, length us, event | category | flops | bytes accessed | tf_op | source)
XLA Modules:
  0.0 642.2 jit_solution(3127442550304720595)
XLA Ops:
  8.0 1.9 pad_maximum_fusion.1
  11.4 2.6 fusion.1
  17.1 99.3 %all-gather.6.cloned.1.call-done = bf16[512,4096]{1,0:T(8,128)(2,1)} async-done(((bf16[512,256]{1,0:T(8,128)(2,1)}), bf16[512,4096]{1,0:T(8,128)(2,1)}) %all-gather.6.cloned.1.call-update) | async-done | bytes 4194320 | tf_op jit(solution)/shard_map/all_gather | solution.py:156
  116.3 4.8 fusion.14
  122.3 140.4 %all-gather.4.cloned.1.call-done = bf16[4096,768]{1,0:T(8,128)(2,1)} async-done(((bf16[256,768]{1,0:T(8,128)(2,1)}), bf16[4096,768]{1,0:T(8,128)(2,1)}) %all-gather.4.cloned.1.call-update) | async-done | bytes 6291472 | tf_op jit(solution)/shard_map/all_gather | solution.py:112
  262.7 6.4 fusion.71
  271.5 2.3 reshape.328
  276.6 4.9 collective-permute-start
  287.9 4.8 fusion.72
  292.7 2.5 fusion.13
  305.9 3.0 collective-permute-done.1
  313.0 7.4 %convolution_convert_fusion.2 = bf16[384,4096]{1,0:T(8,128)(2,1)} fusion(bf16[4096,768]{1,0:T(8,128)(2,1)} %all-gather.4.cloned.1.call-done, bf16[384,128]{0,1:T(8,128)(2,1)} %copy.53, bf16[384,64]{0,1:T(8,128)(2,1)} %copy.52, bf16[384,64]{0,1:T(8,128)(2,1)} %copy.51, bf16[384,512]{0,1:T(8,128)(2,1)} %bitcast.134), kind=kOutput, calls=%fused_computation.7 | convolution fusion | flops 2419851264 | bytes 10027008 | tf_op jit(solution)/shard_map/dot_general | solution.py:80
  320.7 4.3 fusion.2
  325.0 8.4 %convolution_convert_fusion = bf16[4096,768]{1,0:T(8,128)(2,1)} fusion(f32[4096]{0:T(1024)} %param.11, bf16[384,128]{0,1:T(8,128)(2,1)} %copy.53, bf16[384,64]{0,1:T(8,128)(2,1)} %copy.52, bf16[384,64]{0,1:T(8,128)(2,1)} %copy.51, bf16[384,512]{0,1:T(8,128)(2,1)} %bitcast.135, bf16[1,1,384,4096]{3,2,1,0:T(8,128)(2,1)} %param.9, f32[384]{0:T(512)S(1)} %add_rsqrt_fusion), kind=kOutput, calls=%fused_computation.3 | convolution fusion | flops 2427715584 | bytes 10044928 | tf_op jit(solution)/shard_map/dot_general | solution.py:86
  333.5 5.7 convolution_convert_fusion.3
  339.9 5.4 convert_multiply_fusion
  345.3 11.2 %reduce-scatter.7.cloned.1.call-done = bf16[384,512]{1,0:T(8,128)(2,1)} async-done(((bf16[384,4096]{1,0:T(8,128)(2,1)}), bf16[384,512]{1,0:T(8,128)(2,1)}) %reduce-scatter.7.cloned.1.call-update) | async-done | bytes 393232 | tf_op jit(solution)/shard_map/reduce_scatter | solution.py:207
  358.0 34.9 %psum.15 = f32[512]{0:T(512)S(1)} all-reduce(f32[512]{0:T(512)S(1)} %get-tuple-element.7), channel_id=1, replica_groups=mesh['dp'=8,'head'=8,'pair'=2] {'dp','pair'}, use_global_device_ids=true, to_apply=%region_11.12 | all-reduce | flops 512 | bytes 4096 | tf_op jit(solution)/shard_map/psum | solution.py:219
  392.9 20.4 %all-gather = f32[8,1,512]{2,1,0:T(1,128)S(1)} all-gather(f32[1,1,512]{2,1,0:T(1,128)S(1)} %bitcast.137), channel_id=1, replica_groups=mesh['dp'=8,'head'=8,'pair'=2] {'head'}, dimensions={0}, use_global_device_ids=true | all-gather | bytes 18432 | tf_op jit(solution)/shard_map/all_gather | solution.py:220
  413.3 12.4 %psum.14 = f32[384]{0:T(512)S(1)} all-reduce(f32[384]{0:T(512)S(1)} %get-tuple-element.8), channel_id=1, replica_groups=mesh['dp'=8,'head'=8,'pair'=2] {'head'}, use_global_device_ids=true, to_apply=%region_7.8 | all-reduce | flops 384 | bytes 3072 | tf_op jit(solution)/shard_map/psum | solution.py:217
  425.7 2.3 fusion.25
  428.0 28.7 %reduce-scatter.11.cloned.1.call-done = bf16[256,512]{0,1:T(8,128)(2,1)} async-done(((bf16[4096,512]{0,1:T(8,128)(2,1)}), bf16[256,512]{0,1:T(8,128)(2,1)}) %reduce-scatter.11.cloned.1.call-update) | async-done | bytes 262160 | tf_op jit(solution)/shard_map/reduce_scatter | solution.py:168
  458.5 139.4 %reduce-scatter.9.cloned.1.call-done = bf16[256,768]{1,0:T(8,128)(2,1)} async-done(((bf16[4096,768]{1,0:T(8,128)(2,1)}), bf16[256,768]{1,0:T(8,128)(2,1)}) %reduce-scatter.9.cloned.1.call-update) | async-done | bytes 393232 | tf_op jit(solution)/shard_map/reduce_scatter | solution.py:200
  601.3 33.5 %reduce-scatter.5.cloned.1.call-done = bf16[384,512]{1,0:T(8,128)(2,1)} async-done(((bf16[384,4096]{1,0:T(8,128)(2,1)}), bf16[384,512]{1,0:T(8,128)(2,1)}) %reduce-scatter.5.cloned.1.call-update) | async-done | bytes 393232 | tf_op jit(solution)/shard_map/reduce_scatter | solution.py:159
  (107 shorter events, 39.8 us)
Async XLA Ops:
  7.2 109.1 %copy-start = (bf16[1,1,384,4096]{3,2,1,0:T(8,128)(2,1)S(1)}, bf16[1,1,384,4096]{3,2,1,0:T(8,128)(2,1)}, u32[]{:S(2)}) copy-start(bf16[1,1,384,4096]{3,2,1,0:T(8,128)(2,1)} %param.10) | copy-start | bytes 9437188
  7.2 109.1 %all-gather.6.cloned.1.call-start = ((), (), s32[]{:S(2)}) async-start(), calls=%async_computation.5 | async-start | bytes 4456448 | tf_op jit(solution)/shard_map/all_gather | solution.py:156
  7.9 254.8 %all-gather.4.cloned.1.call-start = ((), (), s32[]{:S(2)}) async-start(), calls=%async_computation.4 | async-start | bytes 6684672 | tf_op jit(solution)/shard_map/all_gather | solution.py:112
  9.9 346.6 %reduce-scatter.7.cloned.1.call-start = ((), (), s32[]{:S(2)}) async-start(), calls=%async_computation.7 | async-start | bytes 3538944 | tf_op jit(solution)/shard_map/reduce_scatter | solution.py:207
  11.3 262.4 %copy-start.17 = (f32[64]{0:T(128)}, f32[64]{0:T(128)S(1)}, u32[]{:S(2)}) copy-start(f32[64]{0:T(128)S(1)} %multiply_exponential_fusion) | copy-start | bytes 772
  269.1 1.8 copy-start.16
  273.8 9.7 %copy-start.2 = (f32[384,64]{1,0:T(8,128)S(1)}, f32[384,64]{1,0:T(8,128)}, u32[]{:S(2)}) copy-start(f32[384,64]{1,0:T(8,128)} %get-tuple-element.29) | copy-start | bytes 294916
  273.8 9.7 %copy-start.4 = (f32[384,64]{1,0:T(8,128)S(1)}, f32[384,64]{1,0:T(8,128)}, u32[]{:S(2)}) copy-start(f32[384,64]{1,0:T(8,128)} %get-tuple-element.30) | copy-start | bytes 294916
  273.8 12.8 %copy-start.9 = (bf16[1,256,128]{2,1,0:T(8,128)(2,1)S(1)}, bf16[1,256,128]{2,1,0:T(8,128)(2,1)}, u32[]{:S(2)}) copy-start(bf16[1,256,128]{2,1,0:T(8,128)(2,1)} %slice_bitcast_fusion.7) | copy-start | bytes 196612
  276.6 9.9 %collective-permute-start = (bf16[2,256,128]{2,1,0:T(8,128)(2,1)S(1)}, bf16[2,256,128]{2,1,0:T(8,128)(2,1)S(1)}, u32[]{:S(2)}, u32[]{:S(2)}) collective-permute-start(bf16[2,256,128]{2,1,0:T(8,128)(2,1)S(1)} %pad_maximum_fusion.6), channel_id=1, source_target_pairs={{0,1},{1,0},{2,3},{3,2},{4,5},{5,4},{6,7},{7,6},{8,9},{9,8},{10,11... | collective-permute-start | bytes 393224 | tf_op jit(solution)/shard_map/ppermute | solution.py:22
  292.7 3.9 copy-start.12
  292.7 3.9 copy-start.13
  292.7 3.9 copy-start.15
  295.2 2.7 copy-start.1
  297.9 1.9 copy-start.10
  297.9 1.9 copy-start.11
  297.9 1.9 copy-start.14
  299.0 1.7 copy-start.5
  300.7 9.2 %copy-start.18 = (f32[64]{0:T(128)S(1)}, f32[64]{0:T(128)}, u32[]{:S(2)}) copy-start(f32[64]{0:T(128)} %copy-done.17) | copy-start | bytes 772
  305.0 3.9 collective-permute-start.1
  313.0 7.7 %copy-start.8 = (bf16[384,4,128]{0,2,1:T(8,128)(2,1)S(1)}, bf16[384,4,128]{0,2,1:T(8,128)(2,1)}, u32[]{:S(2)}) copy-start(bf16[384,4,128]{0,2,1:T(8,128)(2,1)} %get-tuple-element.14) | copy-start | bytes 1179652
  320.4 136.3 %reduce-scatter.11.cloned.1.call-start = ((), (), s32[]{:S(2)}) async-start(), calls=%async_computation.9 | async-start | bytes 4456448 | tf_op jit(solution)/shard_map/reduce_scatter | solution.py:168
  325.0 272.9 %reduce-scatter.9.cloned.1.call-start = ((), (), s32[]{:S(2)}) async-start(), calls=%async_computation.8 | async-start | bytes 6684672 | tf_op jit(solution)/shard_map/reduce_scatter | solution.py:200
  333.4 301.3 %reduce-scatter.5.cloned.1.call-start = ((), (), s32[]{:S(2)}) async-start(), calls=%async_computation.6 | async-start | bytes 3538944 | tf_op jit(solution)/shard_map/reduce_scatter | solution.py:159
  (3 other events, 3.8 us)
Sparse Core Ops, SparseCore 0:
  9.6 106.6 all-gather.5
  118.5 144.1 all-gather.3
  320.5 35.9 reduce-scatter.6
  358.8 97.8 reduce-scatter.10
  459.0 138.8 reduce-scatter.8
  600.7 33.9 reduce-scatter.4
where the time goes:
time: 646 us; the launch traced here: 642 us
  waiting for transfers between devices  456 us (71%)
  blocking collectives  67.6 us (10%)
  matrix products  46.8 us (7%)
  other arithmetic  29.9 us (5%)
  local copies, waits for them, and re-layouts  20.5 us (3%)
  between operations  15.8 us (2%)
    all_gather x1, waiting for transfers between devices, shards(): lax.all_gather(w_local, ('dp', 'pair'), axis=0, tiled=True)  140 us
    reduce_scatter x1, waiting for transfers between devices, shards(): lax.psum_scatter(contract_first(part, d_proj).astype(jnp.bfloat16), ('dp'...  139 us
    all_gather x1, waiting for transfers between devices, shards(): lax.all_gather(w_out, ('dp', 'pair'), axis=1, tiled=True)  99.3 us
    psum x1, blocking collectives, shards(): gain_sum = lax.psum(gain_part, ('dp', 'pair'))  34.9 us
    reduce_scatter x1, waiting for transfers between devices, shards(): lax.psum_scatter(partial_out.astype(jnp.bfloat16), 'head', scatter_dimens...  33.5 us
    reduce_scatter x1, waiting for transfers between devices, shards(): lax.psum_scatter(contract_first(part, pieces).astype(jnp.bfloat16), ('dp'...  28.7 us
    all_gather x1, blocking collectives, shards(): grad_gain = lax.all_gather(gain_sum, 'head', axis=0, tiled=True)  20.4 us
  transfers between devices with their start and end apart: 8, of which 7 were waited for; matrix products, arithmetic and copies ran while one was open for 8% of the time, Pallas kernels for 0%

commit v1 on v0

v1 whole, which is shorter than its diff:
```python
import functools

import jax
import jax.numpy as jnp
from jax import lax
from jax.experimental import pallas as pl
from jax.experimental.pallas import tpu as pltpu
from jax.sharding import PartitionSpec as P

HEAD_DIM = 128
HALF = 256
RESP = 128
SLOTS = HALF + RESP
KEYS = 2 * HALF + RESP
EPS = 1e-05
BASE = 500000.0
SCALE = HEAD_DIM ** (-0.5)
GROUP = 4
QC = GROUP * HEAD_DIM
WC = QC + 2 * HEAD_DIM
SHARDS = 16
ROWS = 256
MESH = pl.DeviceIdType.MESH
F32 = jnp.float32
BF16 = jnp.bfloat16
PLANE = 20


def dot_nn(a, b):
    return lax.dot_general(a, b, (((1,), (0,)), ((), ())), preferred_element_type=F32)


def dot_nt(a, b):
    return lax.dot_general(a, b, (((1,), (1,)), ((), ())), preferred_element_type=F32)


def dot_tn(a, b):
    return lax.dot_general(a, b, (((0,), (0,)), ((), ())), preferred_element_type=F32)


def step(value, offset):
    return lax.rem(value + offset % 4, 4)


GROUPS = (
    (1, lambda i: (2, 2)),
    (4, lambda i: ((1 + 2 * lax.rem(i, 2)) * (1 - i // 2) + 2 * (i // 2), 2 * (1 - i // 2) + (1 + 2 * lax.rem(i, 2)) * (i // 2))),
    (2, lambda i: (2 * i, 2 * (1 - i))),
    (4, lambda i: (1 + 2 * lax.rem(i, 2), 1 + 2 * (i // 2))),
    (4, lambda i: ((1 + 2 * lax.rem(i, 2)) * (1 - i // 2), (1 + 2 * lax.rem(i, 2)) * (i // 2))),
    (1, lambda i: (0, 0)),
)


def kernel(
    hidden, d_out, gain, wq, wk, wv, wo, plen, rlen,
    branch, g_hidden, g_wq, g_wk, g_wv, g_wo, g_gain,
    wg, wog, hid, dout, normed, norm_t, go, qa, qb, qc, qd, oa, ob, oc, od,
    p_core, p_za, p_zb, n_core, n_za, n_zb,
    probs, bias, pacc, attf, att, att_t, gatt, qh, kall, vall, cosf, sinf, inv, hslice,
    dproj, dkv, kv_out, kv_in, rstat, gx, gy, gh,
    load_sem, send_sem, recv_sem, core_send, core_recv, small_send, small_recv,
):
    dp, head, pair = lax.axis_index("dp"), lax.axis_index("head"), lax.axis_index("pair")
    x, y = lax.rem(dp, 4), (dp // 4) * 2 + pair
    z, c = head // 2, lax.rem(head, 2)

    def place(px, py):
        return ((py // 2) * 4 + px) * 2 + lax.rem(py, 2)

    def shard(dx, dy):
        return place(lax.rem(x + dx, 4), lax.rem(y + dy, 4))

    def device(px=x, py=y, h=head):
        return ((py // 2) * 4 + px, h, lax.rem(py, 2))

    def along(axis, k):
        if axis == "x":
            return device(px=step(x, k))
        if axis == "y":
            return device(py=step(y, k))
        if axis == "z":
            return device(h=step(z, k) * 2 + c)
        return device(h=z * 2 + (1 - c))

    pending = []

    def sent():
        for copy in pending:
            copy.wait_send()
        pending.clear()

    def start(src, dst, sems, index, target):
        copy = pltpu.make_async_remote_copy(
            src_ref=src, dst_ref=dst, send_sem=sems[0].at[index], recv_sem=sems[1].at[index],
            device_id=target, device_id_type=MESH,
        )
        copy.start()
        pending.append(copy)

    def arrived(dst, sems, index):
        pltpu.make_async_remote_copy(
            src_ref=dst, dst_ref=dst, send_sem=sems[0].at[index], recv_sem=sems[1].at[index],
            device_id=along("x", 1), device_id_type=MESH,
        ).wait_recv()

    plane_sems = (send_sem, recv_sem)
    core_sems = (core_send, core_recv)
    small_sems = (small_send, small_recv)

    def spot(h, a, b):
        return shard(a % 4, b % 4) if h == 0 else shard(b % 4, a % 4)

    def ring(h, primary):
        return "x" if (h == 0) == primary else "y"

    def part(rows, h, s=None):
        if s is None:
            return pl.ds(h * rows // 2, rows // 2)
        return pl.ds(h * rows // 2 + s * rows // 4, rows // 4)

    def gather(buf, t, rows):
        def go_(h, m, a, b, s, primary, k):
            ref = buf.at[spot(h, a, b), part(rows, h, s)]
            start(ref, ref, plane_sems, (t * 2 + h) * PLANE + m, along(ring(h, primary), k))

        def got(h, m, a, b, s=None):
            arrived(buf.at[spot(h, a, b), part(rows, h, s)], plane_sems, (t * 2 + h) * PLANE + m)

        both = (0, 1)
        for h in both:
            go_(h, 0, 0, 0, None, True, 1)
            go_(h, 1, 0, 0, None, True, -1)
        for h in both:
            go_(h, 4, 0, 0, None, False, 1)
            go_(h, 5, 0, 0, None, False, -1)
        yield
        for h in both:
            got(h, 0, -1, 0)
            go_(h, 2, -1, 0, 0, True, 1)
            got(h, 1, 1, 0)
            go_(h, 3, 1, 0, 1, True, -1)
        for h in both:
            for k in (1, 3):
                go_(h, 4 + 4 * k, k, 0, None, False, 1)
                go_(h, 5 + 4 * k, k, 0, None, False, -1)
        yield
        for h in both:
            got(h, 4, 0, -1)
            go_(h, 6, 0, -1, 0, False, 1)
            got(h, 5, 0, 1)
            go_(h, 7, 0, 1, 1, False, -1)
        yield 4
        for h in both:
            got(h, 2, 2, 0, 0)
            got(h, 3, 2, 0, 1)
            go_(h, 12, 2, 0, None, False, 1)
            go_(h, 13, 2, 0, None, False, -1)
        yield
        for k in (1, 3):
            for h in both:
                got(h, 4 + 4 * k, k, -1)
                go_(h, 6 + 4 * k, k, -1, 0, False, 1)
                got(h, 5 + 4 * k, k, 1)
                go_(h, 7 + 4 * k, k, 1, 1, False, -1)
        yield 3
        for h in both:
            got(h, 6, 0, 2, 0)
            got(h, 7, 0, 2, 1)
        yield 2
        for h in both:
            got(h, 12, 2, -1)
            go_(h, 14, 2, -1, 0, False, 1)
            got(h, 13, 2, 1)
            go_(h, 15, 2, 1, 1, False, -1)
        for h in both:
            for k in (1, 3):
                got(h, 6 + 4 * k, k, 2, 0)
                got(h, 7 + 4 * k, k, 2, 1)
        yield 1
        for h in both:
            got(h, 14, 2, 2, 0)
            got(h, 15, 2, 2, 1)
        yield 0

    def reduce(buf, ra, rb, rc, rd, t, rows, finish):
        def send(h, m, a, b, s, dst, primary, k):
            src = buf.at[spot(h, a, b), part(rows, h, s)]
            start(src, dst, plane_sems, (t * 2 + h) * PLANE + m, along(ring(h, primary), k))

        def got(h, m, dst):
            arrived(dst, plane_sems, (t * 2 + h) * PLANE + m)

        def add(h, a, b, s, *terms):
            j, rows_ = spot(h, a, b), part(rows, h, s)
            total = buf[j, rows_].astype(F32)
            for term in terms:
                total = total + term.astype(F32)
            buf[j, rows_] = total.astype(BF16)

        both = (0, 1)

        def begin(k):
            for h in both:
                send(h, 4 + 4 * k, k, 2, 0, ra.at[h, k, 0], False, 1)
                send(h, 5 + 4 * k, k, 2, 1, ra.at[h, k, 1], False, -1)

        def middle(k):
            for h in both:
                for s, way in ((0, 1), (1, -1)):
                    got(h, 4 + 4 * k + s, ra.at[h, k, s])
                    add(h, k, way, s, ra[h, k, s])
                    send(h, 6 + 4 * k + s, k, way, None, rb.at[h, k, s], False, way)

        def close(k):
            for h in both:
                for s in (0, 1):
                    got(h, 6 + 4 * k + s, rb.at[h, k, s])
                add(h, k, 0, None, rb[h, k, 0], rb[h, k, 1])

        begin(2)
        yield
        for k in (1, 3):
            begin(k)
        yield
        middle(2)
        begin(0)
        yield
        for k in (1, 3):
            middle(k)
        yield
        close(2)
        for h in both:
            send(h, 0, 2, 0, 0, rc.at[h, 0], True, 1)
            send(h, 1, 2, 0, 1, rc.at[h, 1], True, -1)
        yield
        middle(0)
        yield
        for k in (1, 3):
            close(k)
        for h in both:
            for s, way in ((0, 1), (1, -1)):
                got(h, s, rc.at[h, s])
                add(h, way, 0, s, rc[h, s])
                send(h, 2 + s, way, 0, None, rd.at[h, s], True, way)
        yield
        for h in both:
            for s in (0, 1):
                got(h, 6 + s, rb.at[h, 0, s])
                got(h, 2 + s, rd.at[h, s])
            total = buf[spot(h, 0, 0), part(rows, h)].astype(F32)
            for term in (rb[h, 0, 0], rb[h, 0, 1], rd[h, 0], rd[h, 1]):
                total = total + term.astype(F32)
            finish(part(rows, h), total)
        yield

    def head_reduce(buf, r_core, r_za, r_zb, t, finish):
        def block(k, core):
            return pl.ds(2 * (step(z, k) * 2 + core), 2)

        def add(k, rows, term):
            buf[block(k, c), rows] = (buf[block(k, c), rows].astype(F32) + term.astype(F32)).astype(BF16)

        every = pl.ds(0, SLOTS)
        sub = (pl.ds(0, SLOTS // 2), pl.ds(SLOTS // 2, SLOTS // 2))
        for k in (2, 1, 3, 0):
            start(buf.at[block(k, 1 - c)], r_core.at[k], core_sems, t * 8 + k, along("core", 1))
        yield
        arrived(r_core.at[2], core_sems, t * 8 + 2)
        add(2, every, r_core[2])
        for s, way in ((0, 1), (1, -1)):
            start(buf.at[block(2, c), sub[s]], r_za.at[s], core_sems, t * 8 + 4 + s, along("z", way))
        yield
        for s, way in ((0, 1), (1, -1)):
            arrived(r_core.at[way % 4], core_sems, t * 8 + way % 4)
            add(way, every, r_core[way % 4])
            arrived(r_za.at[s], core_sems, t * 8 + 4 + s)
            add(way, sub[s], r_za[s])
            start(buf.at[block(way, c)], r_zb.at[s], core_sems, t * 8 + 6 + s, along("z", way))
        yield
        arrived(r_core.at[0], core_sems, t * 8)
        arrived(r_zb.at[0], core_sems, t * 8 + 6)
        arrived(r_zb.at[1], core_sems, t * 8 + 7)
        for i in range(2):
            total = buf[2 * head + i].astype(F32) + r_core[0, i].astype(F32)
            finish(i, total + r_zb[0, i].astype(F32) + r_zb[1, i].astype(F32))
        yield

    def each(group, body):
        count, offsets = GROUPS[group]
        if count == 1:
            body(shard(*offsets(0)))
            return

        @pl.loop(0, count)
        def _(i):
            body(shard(*offsets(i)))

    own = shard(0, 0)
    loads = []
    for n, (src, dst) in enumerate(((hidden, hid), (d_out, dout))):
        for j in range(SHARDS):
            copy = pltpu.make_async_copy(src.at[:, pl.ds(j * ROWS, ROWS)], dst.at[j], load_sem.at[n * SHARDS + j])
            copy.start()
            loads.append(copy)
    barrier = pltpu.get_barrier_semaphore()
    others = [along("x", k) for k in (1, 2, 3)] + [along("y", k) for k in (1, 2, 3)]
    head_others = [device(h=lax.rem(head + k, 8)) for k in range(1, 8)]
    for target in others + head_others:
        pl.semaphore_signal(barrier, inc=1, device_id=target, device_id_type=MESH)
    wg[own, :, 0:QC] = wq[...]
    wg[own, :, QC:QC + HEAD_DIM] = wk[...]
    wg[own, :, QC + HEAD_DIM:] = wv[...]
    wog[own] = wo[...]
    pl.semaphore_wait(barrier, 13)

    w_gather = gather(wg, 0, ROWS)
    o_gather = gather(wog, 1, QC)
    next(w_gather)

    for copy in loads[:SHARDS]:
        copy.wait()
    pacc[:, 0:ROWS] = jnp.zeros((SLOTS, ROWS), F32)

    @pl.loop(0, SHARDS)
    def _(j):
        block = hid[j].astype(F32)
        pacc[:, 0:ROWS] += block * block

    mean = jnp.sum(pacc[:, 0:ROWS], -1, keepdims=True) * (1.0 / (SHARDS * ROWS))
    inv[...] = jnp.broadcast_to(lax.rsqrt(mean + EPS), (SLOTS, ROWS))

    def norm_block(j):
        block = (hid[j].astype(F32) * inv[...] * gain[j]).astype(BF16)
        normed[j] = block
        norm_t[j] = block.T

    @pl.loop(0, SHARDS // 2)
    def _(j):
        norm_block(j)

    next(w_gather)

    @pl.loop(SHARDS // 2, SHARDS)
    def _(j):
        norm_block(j)

    for i in range(2):
        hslice[i] = hid[2 * head + i]

    prompt_length, resp_length = plen[0], rlen[0]
    slot = lax.broadcasted_iota(jnp.int32, (SLOTS, HEAD_DIM), 0)
    lane = lax.broadcasted_iota(jnp.int32, (8, HEAD_DIM), 1)
    entry = jnp.where(lane < HEAD_DIM // 2, lane, lane - HEAD_DIM // 2)
    freqs = jnp.exp(-(entry.astype(F32) * (2.0 / HEAD_DIM)) * jnp.log(jnp.full((8, HEAD_DIM), BASE, F32)))
    position = jnp.where(slot < HALF, pair * HALF + slot, prompt_length + slot - HALF).astype(F32)
    angle = position * freqs[0:1]
    cosf[...] = jnp.cos(angle)
    sign = jnp.where(lane[0:1] < HEAD_DIM // 2, -1.0, 1.0).astype(F32)
    sinf[...] = jnp.sin(angle) * sign
    s_id = lax.broadcasted_iota(jnp.int32, (SLOTS, KEYS), 0)
    t_id = lax.broadcasted_iota(jnp.int32, (SLOTS, KEYS), 1)
    prompt_key = (t_id < 2 * HALF) & (t_id < prompt_length) & ((s_id >= HALF) | (t_id <= pair * HALF + s_id))
    resp_id = t_id - 2 * HALF
    resp_key = (t_id >= 2 * HALF) & (s_id >= HALF) & (resp_id <= s_id - HALF) & (resp_id < resp_length)
    bias[...] = jnp.where(prompt_key | resp_key, 0.0, -1e30).astype(BF16)

    pacc[...] = dot_nn(normed[own], wg[own])

    def project(j):
        pacc[...] += dot_nn(normed[j], wg[j])

    def pump(gen, times=1, body=None):
        for _ in range(times):
            group = next(gen)
            if group is not None and body is not None:
                each(group, body)

    pump(w_gather, 3, project)
    next(o_gather)
    pump(w_gather, 3, project)
    pump(o_gather)

    def rotate(u):
        return u * cosf[...] + pltpu.roll(u, HEAD_DIM // 2, 1) * sinf[...]

    def unrotate(u):
        return u * cosf[...] - pltpu.roll(u, HEAD_DIM // 2, 1) * sinf[...]

    mine = pl.ds(pl.multiple_of(pair * HALF, HALF), HALF)
    theirs = pl.ds(pl.multiple_of((1 - pair) * HALF, HALF), HALF)
    partner = device(py=(y // 2) * 2 + 1 - pair)
    keys = rotate(pacc[:, QC:QC + HEAD_DIM]).astype(BF16)
    values = pacc[:, QC + HEAD_DIM:].astype(BF16)
    kall[mine] = keys[:HALF]
    kall[2 * HALF:] = keys[HALF:]
    vall[mine] = values[:HALF]
    vall[2 * HALF:] = values[HALF:]
    start(kall.at[mine], kall.at[mine], small_sems, 0, partner)
    start(vall.at[mine], vall.at[mine], small_sems, 1, partner)
    for g in range(GROUP):
        qh[g] = rotate(pacc[:, g * HEAD_DIM:(g + 1) * HEAD_DIM]).astype(BF16)
    for copy in loads[SHARDS:]:
        copy.wait()
    gacc = pacc.at[:, 0:QC]
    gacc[...] = dot_nt(dout[own], wog[own])

    def grad_attend(j):
        gacc[...] += dot_nt(dout[j], wog[j])

    pump(o_gather, 1, grad_attend)
    arrived(kall.at[theirs], small_sems, 0)
    arrived(vall.at[theirs], small_sems, 1)

    for g in range(GROUP):
        cols = slice(g * HEAD_DIM, (g + 1) * HEAD_DIM)
        scores = dot_nt(qh[g], kall[...]) * SCALE + bias[...].astype(F32)
        expo = jnp.exp(scores - jnp.max(scores, -1, keepdims=True))
        prob = expo / jnp.sum(expo, -1, keepdims=True)
        probs[g] = prob
        out = dot_nn(prob.astype(BF16), vall[...])
        attf[:, cols] = out
        rounded = out.astype(BF16)
        att[:, cols] = rounded
        att_t[cols, :] = rounded.T
        pump(o_gather, 1, grad_attend)

    def out_term(j):
        go[j] = dot_nn(att_t[...], dout[j]).astype(BF16)

    def out_finish(rows, total):
        g_wo[rows, :] = total

    o_reduce = reduce(go, oa, ob, oc, od, 3, QC, out_finish)
    each(0, out_term)
    next(o_reduce)
    pump(o_gather, 1, grad_attend)
    each(1, out_term)
    next(o_reduce)
    gatt[...] = gacc[...].astype(BF16)
    each(2, out_term)
    next(o_reduce)
    each(3, out_term)
    next(o_reduce)
    each(4, out_term)
    each(5, out_term)

    dkv[...] = jnp.zeros_like(dkv)
    for g in range(GROUP):
        cols = slice(g * HEAD_DIM, (g + 1) * HEAD_DIM)
        g_head = gatt[:, cols]
        prob = probs[g]
        d_prob = dot_nt(g_head, vall[...])
        delta = jnp.sum(g_head.astype(F32) * attf[:, cols], -1, keepdims=True)
        d_score = (prob * (d_prob - delta) * SCALE).astype(BF16)
        dproj[:, cols] = unrotate(dot_nn(d_score, kall[...])).astype(BF16)
        dkv[0] += dot_tn(d_score, qh[g])
        dkv[1] += dot_tn(prob.astype(BF16), g_head)
        next(o_reduce)
    kv_out[0] = dkv[0, theirs].astype(BF16)
    kv_out[1] = dkv[1, theirs].astype(BF16)
    start(kv_out, kv_in, small_sems, 2, partner)

    @pl.loop(0, SHARDS)
    def _(j):
        hid[j] = dot_nn(att[...], wog[j]).astype(BF16)

    def branch_finish(i, total):
        branch[:, i * ROWS:(i + 1) * ROWS] = total.astype(BF16)

    b_reduce = head_reduce(hid, p_core, p_za, p_zb, 0, branch_finish)
    next(b_reduce)
    arrived(kv_in, small_sems, 2)
    d_keys = jnp.concatenate([dkv[0, mine] + kv_in[0].astype(F32), dkv[0, 2 * HALF:]], 0)
    d_values = jnp.concatenate([dkv[1, mine] + kv_in[1].astype(F32), dkv[1, 2 * HALF:]], 0)
    dproj[:, QC:QC + HEAD_DIM] = unrotate(d_keys).astype(BF16)
    dproj[:, QC + HEAD_DIM:] = d_values.astype(BF16)

    def in_term(j):
        normed[j] = dot_nt(dproj[...], wg[j]).astype(BF16)
        wg[j] = dot_nn(norm_t[j], dproj[...]).astype(BF16)

    def in_finish(rows, total):
        g_wq[rows, :] = total[:, 0:QC]
        g_wk[rows, :] = total[:, QC:QC + HEAD_DIM]
        g_wv[rows, :] = total[:, QC + HEAD_DIM:]

    sent()
    w_reduce = reduce(wg, qa, qb, qc, qd, 2, ROWS, in_finish)
    each(0, in_term)
    next(w_reduce)
    each(1, in_term)
    next(w_reduce)
    each(2, in_term)
    next(w_reduce)
    each(3, in_term)
    next(w_reduce)
    next(b_reduce)
    shares = []

    def norm_finish(i, total):
        shares.append(total)

    each(4, in_term)
    each(5, in_term)
    n_reduce = head_reduce(normed, n_core, n_za, n_zb, 1, norm_finish)
    next(n_reduce)
    next(w_reduce)
    next(b_reduce)
    next(w_reduce)
    next(n_reduce)
    next(b_reduce)
    next(n_reduce)
    next(w_reduce)
    next(n_reduce)

    row_part = jnp.zeros((SLOTS, HEAD_DIM), F32)
    for i in range(2):
        scaled = hslice[i].astype(F32) * inv[...]
        gain_part = jnp.sum(shares[i] * scaled, 0, keepdims=True)
        gx[x, :, i * ROWS:(i + 1) * ROWS] = jnp.broadcast_to(gain_part, (8, ROWS))
        prod = shares[i] * gain[2 * head + i]
        g_hidden[:, i * ROWS:(i + 1) * ROWS] = prod
        prod = prod * scaled
        row_part = row_part + prod[:, :HEAD_DIM] + prod[:, HEAD_DIM:]
    row_sum = jnp.sum(row_part.T, 0, keepdims=True)
    rstat[head] = jnp.broadcast_to(row_sum, (8, SLOTS))
    for k in range(1, 8):
        start(rstat.at[head], rstat.at[head], small_sems, 2 + k, head_others[k - 1])
    for k in range(1, 4):
        start(gx.at[x], gx.at[x], small_sems, 9 + k, along("x", k))
    for k in range(1, 8):
        arrived(rstat.at[lax.rem(head + 8 - k, 8)], small_sems, 2 + k)
    total = jnp.sum(rstat[...], 0)[0:1]
    mean = jnp.broadcast_to(total, (HEAD_DIM, SLOTS)).T * (1.0 / (SHARDS * ROWS))
    for i in range(4):
        cols = slice(i * HEAD_DIM, (i + 1) * HEAD_DIM)
        half = slice((i % 2) * HEAD_DIM, (i % 2 + 1) * HEAD_DIM)
        factor = inv[:, half]
        scaled = hslice[i // 2, :, half].astype(F32) * factor
        g_hidden[:, cols] = factor * (g_hidden[:, cols] - scaled * mean)
    for k in range(1, 4):
        arrived(gx.at[step(x, -k)], small_sems, 9 + k)
    gy[y] = jnp.sum(gx[...], 0)
    for k in range(1, 4):
        start(gy.at[y], gy.at[y], small_sems, 12 + k, along("y", k))
    for k in range(1, 4):
        arrived(gy.at[step(y, -k)], small_sems, 12 + k)
    gh[head] = jnp.sum(gy[...], 0)
    for k in range(1, 8):
        start(gh.at[head], gh.at[head], small_sems, 15 + k, head_others[k - 1])
    next(w_reduce)
    for k in range(1, 8):
        arrived(gh.at[lax.rem(head + 8 - k, 8)], small_sems, 15 + k)
    for i in range(8):
        g_gain[i:i + 1, :] = gh[i, 0:1, :]
    sent()


def shards(hidden, d_out, norm_gain, w_query, w_key, w_value, w_out, prompt_len, resp_len):
    vmem = pl.BlockSpec(memory_space=pltpu.VMEM)
    smem = pl.BlockSpec(memory_space=pltpu.SMEM)
    anywhere = pl.BlockSpec(memory_space=pl.ANY)
    big = (SHARDS, SLOTS, ROWS)
    scratch = [
        pltpu.VMEM((SHARDS, ROWS, WC), BF16),
        pltpu.VMEM((SHARDS, QC, ROWS), BF16),
        pltpu.VMEM(big, BF16),
        pltpu.VMEM(big, BF16),
        pltpu.VMEM(big, BF16),
        pltpu.VMEM((SHARDS, ROWS, SLOTS), BF16),
        pltpu.VMEM((SHARDS, QC, ROWS), BF16),
    ]
    for rows, cols in ((ROWS, WC), (QC, ROWS)):
        scratch += [
            pltpu.VMEM((2, 4, 2, rows // 4, cols), BF16),
            pltpu.VMEM((2, 4, 2, rows // 2, cols), BF16),
            pltpu.VMEM((2, 2, rows // 4, cols), BF16),
            pltpu.VMEM((2, 2, rows // 2, cols), BF16),
        ]
    for _ in range(2):
        scratch += [
            pltpu.VMEM((4, 2, SLOTS, ROWS), BF16),
            pltpu.VMEM((2, 2, SLOTS // 2, ROWS), BF16),
            pltpu.VMEM((2, 2, SLOTS, ROWS), BF16),
        ]
    scratch += [
        pltpu.VMEM((GROUP, SLOTS, KEYS), F32),
        pltpu.VMEM((SLOTS, KEYS), BF16),
        pltpu.VMEM((SLOTS, WC), F32),
        pltpu.VMEM((SLOTS, QC), F32),
        pltpu.VMEM((SLOTS, QC), BF16),
        pltpu.VMEM((QC, SLOTS), BF16),
        pltpu.VMEM((SLOTS, QC), BF16),
        pltpu.VMEM((GROUP, SLOTS, HEAD_DIM), BF16),
        pltpu.VMEM((KEYS, HEAD_DIM), BF16),
        pltpu.VMEM((KEYS, HEAD_DIM), BF16),
        pltpu.VMEM((SLOTS, HEAD_DIM), F32),
        pltpu.VMEM((SLOTS, HEAD_DIM), F32),
        pltpu.VMEM((SLOTS, ROWS), F32),
        pltpu.VMEM((2, SLOTS, ROWS), BF16),
        pltpu.VMEM((SLOTS, WC), BF16),
        pltpu.VMEM((2, KEYS, HEAD_DIM), F32),
        pltpu.VMEM((2, HALF, HEAD_DIM), BF16),
        pltpu.VMEM((2, HALF, HEAD_DIM), BF16),
        pltpu.VMEM((8, 8, SLOTS), F32),
        pltpu.VMEM((4, 8, QC), F32),
        pltpu.VMEM((4, 8, QC), F32),
        pltpu.VMEM((8, 8, QC), F32),
        pltpu.SemaphoreType.DMA((2 * SHARDS,)),
        pltpu.SemaphoreType.DMA((8 * PLANE,)),
        pltpu.SemaphoreType.DMA((8 * PLANE,)),
        pltpu.SemaphoreType.DMA((16,)),
        pltpu.SemaphoreType.DMA((16,)),
        pltpu.SemaphoreType.DMA((24,)),
        pltpu.SemaphoreType.DMA((24,)),
    ]
    outs = pl.pallas_call(
        kernel,
        out_shape=(
            jax.ShapeDtypeStruct((SLOTS, QC), BF16),
            jax.ShapeDtypeStruct((SLOTS, QC), F32),
            jax.ShapeDtypeStruct((ROWS, QC), F32),
            jax.ShapeDtypeStruct((ROWS, HEAD_DIM), F32),
            jax.ShapeDtypeStruct((ROWS, HEAD_DIM), F32),
            jax.ShapeDtypeStruct((QC, ROWS), F32),
            jax.ShapeDtypeStruct((8, QC), F32),
        ),
        in_specs=[anywhere, anywhere, vmem, vmem, vmem, vmem, vmem, smem, smem],
        out_specs=(vmem,) * 7,
        scratch_shapes=scratch,
        compiler_params=pltpu.CompilerParams(
            collective_id=0, has_side_effects=True, vmem_limit_bytes=65011712
        ),
        name="attention_step",
    )(
        hidden[0, 0], d_out[0, 0], norm_gain.reshape(SHARDS, 1, ROWS),
        w_query, w_key, w_value, w_out, prompt_len, resp_len[0],
    )
    branch, g_hidden, g_wq, g_wk, g_wv, g_wo, g_gain = outs
    return (branch[None, None], g_hidden[None, None], g_wq, g_wk, g_wv, g_wo, g_gain.reshape(-1))


def solution(mesh):
    in_specs = (
        P("dp", "pair", None, None),
        P("dp", "pair", None, None),
        P(),
        P(("dp", "pair"), "head"),
        P(("dp", "pair"), "head"),
        P(("dp", "pair"), "head"),
        P("head", ("dp", "pair")),
        P("dp"),
        P("dp", "pair"),
    )
    out_specs = (
        P("dp", "pair", None, "head"),
        P("dp", "pair", None, "head"),
        P(("dp", "pair"), "head"),
        P(("dp", "pair"), "head"),
        P(("dp", "pair"), "head"),
        P("head", ("dp", "pair")),
        P(),
    )
    return jax.shard_map(shards, mesh=mesh, in_specs=in_specs, out_specs=out_specs, check_vma=False)
```

time: 646 us -> 169 us (0.26)
  waiting for transfers between devices: 456 us -> 0 us
  Pallas kernels: 0 us -> 158 us
  blocking collectives: 67.6 us -> 0 us
  matrix products: 46.8 us -> 0 us
  other arithmetic: 29.9 us -> 0 us
  between operations: 15.8 us -> 1.96 us
  local copies, waits for them, and re-layouts: 20.5 us -> 9.21 us
    all_gather x2 -> x0, waiting for transfers between devices: 240 us -> none  [the longest x1 140 us: shards(): lax.all_gather(w_local, ('dp', 'pair'), axis=0, tiled=True)]
    reduce_scatter x4 -> x0, waiting for transfers between devices: 213 us -> none  [the longest x1 139 us: shards(): lax.psum_scatter(contract_first(part, d_proj).astype(jnp.bfloat16), ('dp'...]
    pallas_call x0 -> x1, Pallas kernels: none -> 158 us  [shards(): pl.pallas_call(kernel, out_shape=(jax.ShapeDtypeStruct((SLOTS, QC), BF16)...]
    psum x2 -> x0, blocking collectives: 47.2 us -> none  [the longest x1 34.9 us: shards(): gain_sum = lax.psum(gain_part, ('dp', 'pair'))]
    dot_general x11 -> x0, matrix products: 42 us -> none  [the longest x2 12.6 us: contract_first(): lax.dot_general(left, right, (((0,), (0,)), ((), ())), preferred_element_...]
    all_gather x1 -> x0, blocking collectives: 20.4 us -> none  [shards(): grad_gain = lax.all_gather(gain_sum, 'head', axis=0, tiled=True)]
    unnamed x39 -> x13, local copies, waits for them, and re-layouts: 0.92 us -> 9.21 us
    slice x6 -> x0, local copies, waits for them, and re-layouts: 7.6 us -> none  [the longest x1 1.84 us: rotate(): first = values[..., :HEAD_DIM // 2]]
  transfers between devices with their start and end apart: 8 -> 0, of which waited for: 7 -> 0; matrix products, arithmetic and copies ran while one was open for 8% -> 0% of each run, Pallas kernels for 0% -> 0%
where the time goes in v1:
time: 169 us
  Pallas kernels  158 us (93%)
  local copies, waits for them, and re-layouts  9.21 us (5%)
  between operations  1.96 us (1%)
    pallas_call x1, Pallas kernels, shards(): pl.pallas_call(kernel, out_shape=(jax.ShapeDtypeStruct((SLOTS, QC), BF16)...  158 us
    unnamed x13, local copies, waits for them, and re-layouts  9.21 us

profile of v1, /device:TPU:1, one launch (start us, length us, event | category | flops | bytes accessed | tf_op | source)
XLA Modules:
  0.0 169.1 jit_solution(15066091841442499319)
XLA Ops:
  1.9 158.0 %attention_step.1 = (bf16[384,512]{1,0:T(8,128)(2,1)}, f32[384,512]{1,0:T(8,128)}, f32[256,512]{1,0:T(8,128)}, f32[256,128]{1,0:T(8,128)}, f32[256,128]{1,0:T(8,...) custom-call(bf16[384,4096]{1,0:T(8,128)(2,1)} %bitcast.9, bf16[384,4096]{1,0:T(8,128)(2,1)} %bitcast.10, ...), custom_call_target="tpu_custom_call" | custom-call | tf_op jit(solution)/shard_map/attention_step/pallas_call | solution.py:618
  159.9 0.0 copy-start.2
  159.9 0.0 copy-start.1
  159.9 0.0 copy-start
  159.9 1.4 copy.16
  161.3 1.8 %copy.25 = bf16[1,1,384,512]{3,2,1,0:T(8,128)(2,1)} copy(bf16[1,1,384,512]{3,2,1,0:T(8,128)(2,1)} %bitcast.12) | data formatting | bytes 786432
  163.1 2.1 %copy.26 = f32[1,1,384,512]{3,2,1,0:T(8,128)} copy(f32[1,1,384,512]{3,2,1,0:T(8,128)} %bitcast.11) | data formatting | bytes 1572864
  165.2 1.9 %copy.27 = f32[256,512]{1,0:T(8,128)} copy(f32[256,512]{1,0:T(8,128)} %get-tuple-element.30) | data formatting | bytes 1048576
  167.0 0.0 copy-done.2
  167.0 0.7 copy.28
  167.7 0.0 copy-done.1
  167.7 0.7 copy.29
  168.3 0.0 copy-done
  168.3 0.8 copy.30
Async XLA Ops:
  159.9 7.1 %copy-start.2 = (f32[256,128]{1,0:T(8,128)S(1)}, f32[256,128]{1,0:T(8,128)}, u32[]{:S(2)}) copy-start(f32[256,128]{1,0:T(8,128)} %get-tuple-element.31) | copy-start | bytes 393220
  159.9 7.8 %copy-start.1 = (f32[256,128]{1,0:T(8,128)S(1)}, f32[256,128]{1,0:T(8,128)}, u32[]{:S(2)}) copy-start(f32[256,128]{1,0:T(8,128)} %get-tuple-element.32) | copy-start | bytes 393220
  159.9 8.4 %copy-start = (f32[512,256]{1,0:T(8,128)S(1)}, f32[512,256]{1,0:T(8,128)}, u32[]{:S(2)}) copy-start(f32[512,256]{1,0:T(8,128)} %get-tuple-element.33) | copy-start | bytes 1572868

commit v2 on v1

--- a/solution.py
+++ b/solution.py
@@ -55,7 +55,8 @@
 def kernel(
     hidden, d_out, gain, wq, wk, wv, wo, plen, rlen,
     branch, g_hidden, g_wq, g_wk, g_wv, g_wo, g_gain,
-    wg, wog, hid, dout, normed, norm_t, go, qa, qb, qc, qd, oa, ob, oc, od,
+    wg, wog, hid, dout, normed, norm_t, go, gkv,
+    oa, ob, oc, od, qa, qb, qc, qd, va, vb, vc, vd,
     p_core, p_za, p_zb, n_core, n_za, n_zb,
     probs, bias, pacc, attf, att, att_t, gatt, qh, kall, vall, cosf, sinf, inv, hslice,
     dproj, dkv, kv_out, kv_in, rstat, gx, gy, gh,
@@ -183,108 +184,108 @@
             got(h, 15, 2, 2, 1)
         yield 0
 
-    def reduce(buf, ra, rb, rc, rd, t, rows, finish):
-        def send(h, m, a, b, s, dst, primary, k):
-            src = buf.at[spot(h, a, b), part(rows, h, s)]
-            start(src, dst, plane_sems, (t * 2 + h) * PLANE + m, along(ring(h, primary), k))
-
-        def got(h, m, dst):
-            arrived(dst, plane_sems, (t * 2 + h) * PLANE + m)
-
-        def add(h, a, b, s, *terms):
-            j, rows_ = spot(h, a, b), part(rows, h, s)
-            total = buf[j, rows_].astype(F32)
+    class Reduce:
+        def __init__(self, buf, ra, rb, rc, rd, t, rows, finish, halves=(0, 1)):
+            self.buf, self.ra, self.rb, self.rc, self.rd = buf, ra, rb, rc, rd
+            self.t, self.rows, self.write, self.halves = t, rows, finish, halves
+
+        def send(self, h, m, a, b, s, dst, primary, k):
+            src = self.buf.at[spot(h, a, b), part(self.rows, h, s)]
+            start(src, dst, plane_sems, (self.t * 2 + h) * PLANE + m, along(ring(h, primary), k))
+
+        def got(self, h, m, dst):
+            arrived(dst, plane_sems, (self.t * 2 + h) * PLANE + m)
+
+        def add(self, h, a, b, s, *terms):
+            j, rows = spot(h, a, b), part(self.rows, h, s)
+            total = self.buf[j, rows].astype(F32)
             for term in terms:
                 total = total + term.astype(F32)
-            buf[j, rows_] = total.astype(BF16)
-
-        both = (0, 1)
-
-        def begin(k):
-            for h in both:
-                send(h, 4 + 4 * k, k, 2, 0, ra.at[h, k, 0], False, 1)
-                send(h, 5 + 4 * k, k, 2, 1, ra.at[h, k, 1], False, -1)
-
-        def middle(k):
-            for h in both:
+            self.buf[j, rows] = total.astype(BF16)
+
+        def begin(self, *ks):
+            for k in ks:
+                for h in self.halves:
+                    self.send(h, 4 + 4 * k, k, 2, 0, self.ra.at[h, k, 0], False, 1)
+                    self.send(h, 5 + 4 * k, k, 2, 1, self.ra.at[h, k, 1], False, -1)
+
+        def middle(self, *ks):
+            for k in ks:
+                for h in self.halves:
+                    for s, way in ((0, 1), (1, -1)):
+                        self.got(h, 4 + 4 * k + s, self.ra.at[h, k, s])
+                        self.add(h, k, way, s, self.ra[h, k, s])
+                        self.send(h, 6 + 4 * k + s, k, way, None, self.rb.at[h, k, s], False, way)
+
+        def close(self, *ks):
+            for k in ks:
+                for h in self.halves:
+                    for s in (0, 1):
+                        self.got(h, 6 + 4 * k + s, self.rb.at[h, k, s])
+                    self.add(h, k, 0, None, self.rb[h, k, 0], self.rb[h, k, 1])
+                    if k == 2:
+                        self.send(h, 0, 2, 0, 0, self.rc.at[h, 0], True, 1)
+                        self.send(h, 1, 2, 0, 1, self.rc.at[h, 1], True, -1)
+
+        def cross(self):
+            for h in self.halves:
                 for s, way in ((0, 1), (1, -1)):
-                    got(h, 4 + 4 * k + s, ra.at[h, k, s])
-                    add(h, k, way, s, ra[h, k, s])
-                    send(h, 6 + 4 * k + s, k, way, None, rb.at[h, k, s], False, way)
-
-        def close(k):
-            for h in both:
+                    self.got(h, s, self.rc.at[h, s])
+                    self.add(h, way, 0, s, self.rc[h, s])
+                    self.send(h, 2 + s, way, 0, None, self.rd.at[h, s], True, way)
+
+        def finish(self):
+            for h in self.halves:
                 for s in (0, 1):
-                    got(h, 6 + 4 * k + s, rb.at[h, k, s])
-                add(h, k, 0, None, rb[h, k, 0], rb[h, k, 1])
-
-        begin(2)
-        yield
-        for k in (1, 3):
-            begin(k)
-        yield
-        middle(2)
-        begin(0)
-        yield
-        for k in (1, 3):
-            middle(k)
-        yield
-        close(2)
-        for h in both:
-            send(h, 0, 2, 0, 0, rc.at[h, 0], True, 1)
-            send(h, 1, 2, 0, 1, rc.at[h, 1], True, -1)
-        yield
-        middle(0)
-        yield
-        for k in (1, 3):
-            close(k)
-        for h in both:
-            for s, way in ((0, 1), (1, -1)):
-                got(h, s, rc.at[h, s])
-                add(h, way, 0, s, rc[h, s])
-                send(h, 2 + s, way, 0, None, rd.at[h, s], True, way)
-        yield
-        for h in both:
-            for s in (0, 1):
-                got(h, 6 + s, rb.at[h, 0, s])
-                got(h, 2 + s, rd.at[h, s])
-            total = buf[spot(h, 0, 0), part(rows, h)].astype(F32)
-            for term in (rb[h, 0, 0], rb[h, 0, 1], rd[h, 0], rd[h, 1]):
-                total = total + term.astype(F32)
-            finish(part(rows, h), total)
-        yield
-
-    def head_reduce(buf, r_core, r_za, r_zb, t, finish):
-        def block(k, core):
-            return pl.ds(2 * (step(z, k) * 2 + core), 2)
-
-        def add(k, rows, term):
-            buf[block(k, c), rows] = (buf[block(k, c), rows].astype(F32) + term.astype(F32)).astype(BF16)
-
-        every = pl.ds(0, SLOTS)
-        sub = (pl.ds(0, SLOTS // 2), pl.ds(SLOTS // 2, SLOTS // 2))
-        for k in (2, 1, 3, 0):
-            start(buf.at[block(k, 1 - c)], r_core.at[k], core_sems, t * 8 + k, along("core", 1))
-        yield
-        arrived(r_core.at[2], core_sems, t * 8 + 2)
-        add(2, every, r_core[2])
-        for s, way in ((0, 1), (1, -1)):
-            start(buf.at[block(2, c), sub[s]], r_za.at[s], core_sems, t * 8 + 4 + s, along("z", way))
-        yield
-        for s, way in ((0, 1), (1, -1)):
-            arrived(r_core.at[way % 4], core_sems, t * 8 + way % 4)
-            add(way, every, r_core[way % 4])
-            arrived(r_za.at[s], core_sems, t * 8 + 4 + s)
-            add(way, sub[s], r_za[s])
-            start(buf.at[block(way, c)], r_zb.at[s], core_sems, t * 8 + 6 + s, along("z", way))
-        yield
-        arrived(r_core.at[0], core_sems, t * 8)
-        arrived(r_zb.at[0], core_sems, t * 8 + 6)
-        arrived(r_zb.at[1], core_sems, t * 8 + 7)
-        for i in range(2):
-            total = buf[2 * head + i].astype(F32) + r_core[0, i].astype(F32)
-            finish(i, total + r_zb[0, i].astype(F32) + r_zb[1, i].astype(F32))
-        yield
+                    self.got(h, 6 + s, self.rb.at[h, 0, s])
+                    self.got(h, 2 + s, self.rd.at[h, s])
+                total = self.buf[spot(h, 0, 0), part(self.rows, h)].astype(F32)
+                for term in (self.rb[h, 0, 0], self.rb[h, 0, 1], self.rd[h, 0], self.rd[h, 1]):
+                    total = total + term.astype(F32)
+                self.write(h, total)
+
+    class HeadReduce:
+        def __init__(self, buf, r_core, r_za, r_zb, t):
+            self.buf, self.r_core, self.r_za, self.r_zb, self.base = buf, r_core, r_za, r_zb, t * 12
+
+        def block(self, k, core):
+            return 2 * (step(z, k) * 2 + core)
+
+        def add(self, k, i, rows, term):
+            j = self.block(k, c) + i
+            self.buf[j, rows] = (self.buf[j, rows].astype(F32) + term.astype(F32)).astype(BF16)
+
+        def swap(self, k):
+            start(self.buf.at[pl.ds(self.block(k, 1 - c), 2)], self.r_core.at[k], core_sems, self.base + k, along("core", 1))
+
+        def begin(self):
+            arrived(self.r_core.at[2], core_sems, self.base + 2)
+            for i in range(2):
+                self.add(2, i, pl.ds(0, SLOTS), self.r_core[2, i])
+                for s, way in ((0, 1), (1, -1)):
+                    rows = pl.ds(s * SLOTS // 2, SLOTS // 2)
+                    src = self.buf.at[self.block(2, c) + i, rows]
+                    start(src, self.r_za.at[s, i], core_sems, self.base + 4 + 2 * s + i, along("z", way))
+
+        def middle(self):
+            for way in (1, -1):
+                arrived(self.r_core.at[way % 4], core_sems, self.base + way % 4)
+                for i in range(2):
+                    self.add(way, i, pl.ds(0, SLOTS), self.r_core[way % 4, i])
+            for i in range(2):
+                for s, way in ((0, 1), (1, -1)):
+                    arrived(self.r_za.at[s, i], core_sems, self.base + 4 + 2 * s + i)
+                    self.add(way, i, pl.ds(s * SLOTS // 2, SLOTS // 2), self.r_za[s, i])
+                    src = self.buf.at[self.block(way, c) + i]
+                    start(src, self.r_zb.at[s, i], core_sems, self.base + 8 + 2 * s + i, along("z", way))
+
+        def total(self, i):
+            if i == 0:
+                arrived(self.r_core.at[0], core_sems, self.base)
+            for s in range(2):
+                arrived(self.r_zb.at[s, i], core_sems, self.base + 8 + 2 * s + i)
+            own_term = self.buf[2 * head + i].astype(F32) + self.r_core[0, i].astype(F32)
+            return own_term + self.r_zb[0, i].astype(F32) + self.r_zb[1, i].astype(F32)
 
     def each(group, body):
         count, offsets = GROUPS[group]
@@ -335,16 +336,9 @@
         normed[j] = block
         norm_t[j] = block.T
 
-    @pl.loop(0, SHARDS // 2)
+    @pl.loop(0, SHARDS)
     def _(j):
         norm_block(j)
-
-    next(w_gather)
-
-    @pl.loop(SHARDS // 2, SHARDS)
-    def _(j):
-        norm_block(j)
-
     for i in range(2):
         hslice[i] = hid[2 * head + i]
 
@@ -365,6 +359,7 @@
     resp_key = (t_id >= 2 * HALF) & (s_id >= HALF) & (resp_id <= s_id - HALF) & (resp_id < resp_length)
     bias[...] = jnp.where(prompt_key | resp_key, 0.0, -1e30).astype(BF16)
 
+    next(w_gather)
     pacc[...] = dot_nn(normed[own], wg[own])
 
     def project(j):
@@ -376,10 +371,12 @@
             if group is not None and body is not None:
                 each(group, body)
 
-    pump(w_gather, 3, project)
-    next(o_gather)
-    pump(w_gather, 3, project)
-    pump(o_gather)
+    early = []
+    for which in "wwwwwow":
+        if which == "w":
+            pump(w_gather, 1, project)
+        else:
+            early.append(next(o_gather))
 
     def rotate(u):
         return u * cosf[...] + pltpu.roll(u, HEAD_DIM // 2, 1) * sinf[...]
@@ -408,7 +405,16 @@
     def grad_attend(j):
         gacc[...] += dot_nt(dout[j], wog[j])
 
-    pump(o_gather, 1, grad_attend)
+    def branch_term(j):
+        hid[j] = dot_nn(att[...], wog[j]).astype(BF16)
+
+    def out_term(j):
+        go[j] = dot_nn(att_t[...], dout[j]).astype(BF16)
+
+    for group in early:
+        if group is not None:
+            each(group, grad_attend)
+    pump(o_gather, 2, grad_attend)
     arrived(kall.at[theirs], small_sems, 0)
     arrived(vall.at[theirs], small_sems, 1)
 
@@ -423,30 +429,28 @@
         rounded = out.astype(BF16)
         att[:, cols] = rounded
         att_t[cols, :] = rounded.T
-        pump(o_gather, 1, grad_attend)
-
-    def out_term(j):
-        go[j] = dot_nn(att_t[...], dout[j]).astype(BF16)
-
-    def out_finish(rows, total):
-        g_wo[rows, :] = total
-
-    o_reduce = reduce(go, oa, ob, oc, od, 3, QC, out_finish)
+        pump(o_gather, (1, 1, 1, 1)[g], grad_attend)
+
+    def out_finish(h, total):
+        g_wo[h * ROWS:(h + 1) * ROWS, :] = total
+
+    out = Reduce(go, oa, ob, oc, od, 3, QC, out_finish)
+    branch_sum = HeadReduce(hid, p_core, p_za, p_zb, 0)
     each(0, out_term)
-    next(o_reduce)
+    out.begin(2)
+    each(1, out_term)
+    out.begin(1, 3)
+    each(2, out_term)
+    out.begin(0)
+    each(3, out_term)
     pump(o_gather, 1, grad_attend)
-    each(1, out_term)
-    next(o_reduce)
     gatt[...] = gacc[...].astype(BF16)
-    each(2, out_term)
-    next(o_reduce)
-    each(3, out_term)
-    next(o_reduce)
-    each(4, out_term)
-    each(5, out_term)
+    gather_sent = list(pending)
+    out.middle(2)
 
     dkv[...] = jnp.zeros_like(dkv)
-    for g in range(GROUP):
+
+    def backward(g):
         cols = slice(g * HEAD_DIM, (g + 1) * HEAD_DIM)
         g_head = gatt[:, cols]
         prob = probs[g]
@@ -456,63 +460,97 @@
         dproj[:, cols] = unrotate(dot_nn(d_score, kall[...])).astype(BF16)
         dkv[0] += dot_tn(d_score, qh[g])
         dkv[1] += dot_tn(prob.astype(BF16), g_head)
-        next(o_reduce)
+
+    backward(0)
+    backward(1)
+    each(4, out_term)
+    out.middle(1, 3)
+    backward(2)
+    backward(3)
     kv_out[0] = dkv[0, theirs].astype(BF16)
     kv_out[1] = dkv[1, theirs].astype(BF16)
     start(kv_out, kv_in, small_sems, 2, partner)
+    out.middle(0)
+    each(5, out_term)
 
     @pl.loop(0, SHARDS)
     def _(j):
-        hid[j] = dot_nn(att[...], wog[j]).astype(BF16)
-
-    def branch_finish(i, total):
-        branch[:, i * ROWS:(i + 1) * ROWS] = total.astype(BF16)
-
-    b_reduce = head_reduce(hid, p_core, p_za, p_zb, 0, branch_finish)
-    next(b_reduce)
+        branch_term(j)
+
+    for k in (2, 1, 3, 0):
+        branch_sum.swap(k)
+
+    for copy in gather_sent:
+        copy.wait_send()
+        pending.remove(copy)
+
+    def query_term(j):
+        for h in range(2):
+            wog[j, h * ROWS:(h + 1) * ROWS] = dot_nn(norm_t[j], dproj[:, h * ROWS:(h + 1) * ROWS]).astype(BF16)
+
+    def kv_term(j):
+        gkv[j] = dot_nn(norm_t[j], dproj[:, QC:]).astype(BF16)
+
+    def query_finish(h, total):
+        g_wq[:, h * ROWS:(h + 1) * ROWS] = total
+
+    def kv_finish(h, total):
+        rows = slice(h * ROWS // 2, (h + 1) * ROWS // 2)
+        g_wk[rows, :] = total[:, :HEAD_DIM]
+        g_wv[rows, :] = total[:, HEAD_DIM:]
+
+    query = Reduce(wog, qa, qb, qc, qd, 2, QC, query_finish)
+    kv = Reduce(gkv, va, vb, vc, vd, 4, ROWS, kv_finish)
+    each(0, query_term)
+    query.begin(2)
+    each(1, query_term)
+    query.begin(1, 3)
     arrived(kv_in, small_sems, 2)
     d_keys = jnp.concatenate([dkv[0, mine] + kv_in[0].astype(F32), dkv[0, 2 * HALF:]], 0)
     d_values = jnp.concatenate([dkv[1, mine] + kv_in[1].astype(F32), dkv[1, 2 * HALF:]], 0)
     dproj[:, QC:QC + HEAD_DIM] = unrotate(d_keys).astype(BF16)
     dproj[:, QC + HEAD_DIM:] = d_values.astype(BF16)
 
-    def in_term(j):
-        normed[j] = dot_nt(dproj[...], wg[j]).astype(BF16)
-        wg[j] = dot_nn(norm_t[j], dproj[...]).astype(BF16)
-
-    def in_finish(rows, total):
-        g_wq[rows, :] = total[:, 0:QC]
-        g_wk[rows, :] = total[:, QC:QC + HEAD_DIM]
-        g_wv[rows, :] = total[:, QC + HEAD_DIM:]
-
-    sent()
-    w_reduce = reduce(wg, qa, qb, qc, qd, 2, ROWS, in_finish)
-    each(0, in_term)
-    next(w_reduce)
-    each(1, in_term)
-    next(w_reduce)
-    each(2, in_term)
-    next(w_reduce)
-    each(3, in_term)
-    next(w_reduce)
-    next(b_reduce)
-    shares = []
-
-    def norm_finish(i, total):
-        shares.append(total)
-
-    each(4, in_term)
-    each(5, in_term)
-    n_reduce = head_reduce(normed, n_core, n_za, n_zb, 1, norm_finish)
-    next(n_reduce)
-    next(w_reduce)
-    next(b_reduce)
-    next(w_reduce)
-    next(n_reduce)
-    next(b_reduce)
-    next(n_reduce)
-    next(w_reduce)
-    next(n_reduce)
+    norm_sum = HeadReduce(normed, n_core, n_za, n_zb, 1)
+
+    def norm_terms(k):
+        first = 4 * step(z, k)
+
+        @pl.loop(0, 4)
+        def _(i):
+            normed[first + i] = dot_nt(dproj[...], wg[first + i]).astype(BF16)
+        norm_sum.swap(k)
+
+    norm_terms(2)
+    norm_terms(1)
+    norm_terms(3)
+    norm_sum.begin()
+    out.close(2)
+    norm_terms(0)
+    each(2, query_term)
+    query.begin(0)
+    query.middle(2)
+    each(3, query_term)
+    query.middle(1, 3)
+    norm_sum.middle()
+    branch_sum.begin()
+    out.close(1, 3)
+    out.cross()
+    each(0, kv_term)
+    kv.begin(2)
+    each(1, kv_term)
+    kv.begin(1, 3)
+    each(4, query_term)
+    query.middle(0)
+    each(5, query_term)
+    query.close(2)
+    each(2, kv_term)
+    kv.begin(0)
+    each(3, kv_term)
+    kv.middle(2)
+    branch_sum.middle()
+    out.finish()
+    shares = [norm_sum.total(i) for i in range(2)]
 
     row_part = jnp.zeros((SLOTS, HEAD_DIM), F32)
     for i in range(2):
@@ -529,6 +567,18 @@
         start(rstat.at[head], rstat.at[head], small_sems, 2 + k, head_others[k - 1])
     for k in range(1, 4):
         start(gx.at[x], gx.at[x], small_sems, 9 + k, along("x", k))
+    kv.middle(1, 3)
+    each(4, kv_term)
+    kv.middle(0)
+    each(5, kv_term)
+    for k in range(1, 4):
+        arrived(gx.at[step(x, -k)], small_sems, 9 + k)
+    gy[y] = jnp.sum(gx[...], 0)
+    for k in range(1, 4):
+        start(gy.at[y], gy.at[y], small_sems, 12 + k, along("y", k))
+    query.close(1, 3)
+    query.cross()
+    kv.close(2)
     for k in range(1, 8):
         arrived(rstat.at[lax.rem(head + 8 - k, 8)], small_sems, 2 + k)
     total = jnp.sum(rstat[...], 0)[0:1]
@@ -540,21 +590,37 @@
         scaled = hslice[i // 2, :, half].astype(F32) * factor
         g_hidden[:, cols] = factor * (g_hidden[:, cols] - scaled * mean)
     for k in range(1, 4):
-        arrived(gx.at[step(x, -k)], small_sems, 9 + k)
-    gy[y] = jnp.sum(gx[...], 0)
-    for k in range(1, 4):
-        start(gy.at[y], gy.at[y], small_sems, 12 + k, along("y", k))
-    for k in range(1, 4):
         arrived(gy.at[step(y, -k)], small_sems, 12 + k)
     gh[head] = jnp.sum(gy[...], 0)
     for k in range(1, 8):
         start(gh.at[head], gh.at[head], small_sems, 15 + k, head_others[k - 1])
-    next(w_reduce)
+    for i in range(2):
+        branch[:, i * ROWS:(i + 1) * ROWS] = branch_sum.total(i).astype(BF16)
+    kv.close(1, 3)
+    kv.cross()
+    query.finish()
+    kv.finish()
     for k in range(1, 8):
         arrived(gh.at[lax.rem(head + 8 - k, 8)], small_sems, 15 + k)
     for i in range(8):
-        g_gain[i:i + 1, :] = gh[i, 0:1, :]
+        g_gain[:, i * QC:(i + 1) * QC] = gh[i, 0:1, :]
     sent()
+
+
+def place_kernel(*refs):
+    count = len(refs) // 3
+    sems = refs[-1]
+    loads, stores = [], []
+    for i in range(count):
+        loads.append(pltpu.make_async_copy(refs[i], refs[2 * count + i], sems.at[i]))
+        stores.append(pltpu.make_async_copy(refs[2 * count + i], refs[count + i], sems.at[count + i]))
+    for load in loads:
+        load.start()
+    for load, store in zip(loads, stores):
+        load.wait()
+        store.start()
+    for store in stores:
+        store.wait()
 
 
 def shards(hidden, d_out, norm_gain, w_query, w_key, w_value, w_out, prompt_len, resp_len):
@@ -570,8 +636,9 @@
         pltpu.VMEM(big, BF16),
         pltpu.VMEM((SHARDS, ROWS, SLOTS), BF16),
         pltpu.VMEM((SHARDS, QC, ROWS), BF16),
+        pltpu.VMEM((SHARDS, ROWS, ROWS), BF16),
     ]
-    for rows, cols in ((ROWS, WC), (QC, ROWS)):
+    for rows, cols in ((QC, ROWS), (QC, ROWS), (ROWS, ROWS)):
         scratch += [
             pltpu.VMEM((2, 4, 2, rows // 4, cols), BF16),
             pltpu.VMEM((2, 4, 2, rows // 2, cols), BF16),
@@ -608,10 +675,10 @@
         pltpu.VMEM((4, 8, QC), F32),
         pltpu.VMEM((8, 8, QC), F32),
         pltpu.SemaphoreType.DMA((2 * SHARDS,)),
-        pltpu.SemaphoreType.DMA((8 * PLANE,)),
-        pltpu.SemaphoreType.DMA((8 * PLANE,)),
-        pltpu.SemaphoreType.DMA((16,)),
-        pltpu.SemaphoreType.DMA((16,)),
+        pltpu.SemaphoreType.DMA((10 * PLANE,)),
+        pltpu.SemaphoreType.DMA((10 * PLANE,)),
+        pltpu.SemaphoreType.DMA((24,)),
+        pltpu.SemaphoreType.DMA((24,)),
         pltpu.SemaphoreType.DMA((24,)),
         pltpu.SemaphoreType.DMA((24,)),
     ]
@@ -624,7 +691,7 @@
             jax.ShapeDtypeStruct((ROWS, HEAD_DIM), F32),
             jax.ShapeDtypeStruct((ROWS, HEAD_DIM), F32),
             jax.ShapeDtypeStruct((QC, ROWS), F32),
-            jax.ShapeDtypeStruct((8, QC), F32),
+            jax.ShapeDtypeStruct((1, 8 * QC), F32),
         ),
         in_specs=[anywhere, anywhere, vmem, vmem, vmem, vmem, vmem, smem, smem],
         out_specs=(vmem,) * 7,
@@ -637,7 +704,14 @@
         hidden[0, 0], d_out[0, 0], norm_gain.reshape(SHARDS, 1, ROWS),
         w_query, w_key, w_value, w_out, prompt_len, resp_len[0],
     )
-    branch, g_hidden, g_wq, g_wk, g_wv, g_wo, g_gain = outs
+    branch, g_hidden, g_wq, g_wk, g_wv, g_wo, g_gain = pl.pallas_call(
+        place_kernel,
+        out_shape=tuple(jax.ShapeDtypeStruct(out.shape, out.dtype) for out in outs),
+        in_specs=[anywhere] * 7,
+        out_specs=(anywhere,) * 7,
+        scratch_shapes=[pltpu.VMEM(out.shape, out.dtype) for out in outs] + [pltpu.SemaphoreType.DMA((14,))],
+        name="place_results",
+    )(*outs)
     return (branch[None, None], g_hidden[None, None], g_wq, g_wk, g_wv, g_wo, g_gain.reshape(-1))
 
 

time: 169 us -> 139 us (0.82)
  Pallas kernels: 158 us -> 137 us
  local copies, waits for them, and re-layouts: 9.21 us -> 0 us
    pallas_call x1, Pallas kernels: 158 us -> 134 us  [shards(): pl.pallas_call(kernel, out_shape=(jax.ShapeDtypeStruct((SLOTS, QC), BF16)...]
    unnamed x13 -> x0, local copies, waits for them, and re-layouts: 9.21 us -> none
    pallas_call x0 -> x1, Pallas kernels: none -> 2.69 us  [shards(): pl.pallas_call(place_kernel, out_shape=tuple((jax.ShapeDtypeStruct(out.sh...]
where the time goes in v2:
time: 139 us
  Pallas kernels  137 us (99%)
  between operations  2.1 us (2%)
    pallas_call x1, Pallas kernels, shards(): pl.pallas_call(kernel, out_shape=(jax.ShapeDtypeStruct((SLOTS, QC), BF16)...  134 us

profile of v2, /device:TPU:1, one launch (start us, length us, event | category | flops | bytes accessed | tf_op | source)
XLA Modules:
  0.0 138.8 jit_solution(11781958690381729742)
XLA Ops:
  1.9 134.1 %attention_step.1 = (bf16[384,512]{1,0:T(8,128)(2,1)}, f32[384,512]{1,0:T(8,128)}, f32[256,512]{1,0:T(8,128)}, f32[256,128]{1,0:T(8,128)}, f32[256,128]{1,0:T(8,...) custom-call(bf16[384,4096]{1,0:T(8,128)(2,1)} %bitcast.8, bf16[384,4096]{1,0:T(8,128)(2,1)} %bitcast.9, ...), custom_call_target="tpu_custom_call" | custom-call | tf_op jit(solution)/shard_map/attention_step/pallas_call | solution.py:685
  136.0 2.7 %place_results.1 = (bf16[384,512]{1,0:T(8,128)(2,1)}, f32[384,512]{1,0:T(8,128)}, f32[256,512]{1,0:T(8,128)}, f32[256,128]{1,0:T(8,128)}, f32[256,128]{1,0:T(8,1...) custom-call(bf16[384,512]{1,0:T(8,128)(2,1)} %get-tuple-element.21.refs_0_, f32[384,512]{1,0:T(8,128)} %get-tuple-element.22.refs_1_, ...), custom_call_target="tpu_custom_call" | custom-call | tf_op jit(solution)/shard_map/place_results/pallas_call | solution.py:707

commit v3 on v2

--- a/solution.py
+++ b/solution.py
@@ -24,6 +24,7 @@
 F32 = jnp.float32
 BF16 = jnp.bfloat16
 PLANE = 20
+KV_CUT = 64
 
 
 def dot_nn(a, b):
@@ -54,13 +55,14 @@
 
 def kernel(
     hidden, d_out, gain, wq, wk, wv, wo, plen, rlen,
+    branch_out, g_hidden_out, g_wq_out, g_wk_out, g_wv_out, g_wo_out, g_gain_out,
     branch, g_hidden, g_wq, g_wk, g_wv, g_wo, g_gain,
     wg, wog, hid, dout, normed, norm_t, go, gkv,
     oa, ob, oc, od, qa, qb, qc, qd, va, vb, vc, vd,
     p_core, p_za, p_zb, n_core, n_za, n_zb,
-    probs, bias, pacc, attf, att, att_t, gatt, qh, kall, vall, cosf, sinf, inv, hslice,
+    probs, bias, pacc, gacc, attf, att, att_t, gatt, qh, kall, vall, cosf, sinf, inv, hslice,
     dproj, dkv, kv_out, kv_in, rstat, gx, gy, gh,
-    load_sem, send_sem, recv_sem, core_send, core_recv, small_send, small_recv,
+    load_sem, store_sem, send_sem, recv_sem, core_send, core_recv, small_send, small_recv,
 ):
     dp, head, pair = lax.axis_index("dp"), lax.axis_index("head"), lax.axis_index("pair")
     x, y = lax.rem(dp, 4), (dp // 4) * 2 + pair
@@ -84,7 +86,7 @@
             return device(h=step(z, k) * 2 + c)
         return device(h=z * 2 + (1 - c))
 
-    pending = []
+    pending, gathers = [], []
 
     def sent():
         for copy in pending:
@@ -98,6 +100,7 @@
         )
         copy.start()
         pending.append(copy)
+        return copy
 
     def arrived(dst, sems, index):
         pltpu.make_async_remote_copy(
@@ -115,15 +118,18 @@
     def ring(h, primary):
         return "x" if (h == 0) == primary else "y"
 
-    def part(rows, h, s=None):
+    def part(rows, h, s=None, cut=None):
+        cut = rows // 2 if cut is None else cut
+        first, count = (0, cut) if h == 0 else (cut, rows - cut)
         if s is None:
-            return pl.ds(h * rows // 2, rows // 2)
-        return pl.ds(h * rows // 2 + s * rows // 4, rows // 4)
+            return pl.ds(first, count)
+        return pl.ds(first + s * count // 2, count // 2)
 
     def gather(buf, t, rows):
         def go_(h, m, a, b, s, primary, k):
             ref = buf.at[spot(h, a, b), part(rows, h, s)]
             start(ref, ref, plane_sems, (t * 2 + h) * PLANE + m, along(ring(h, primary), k))
+            gathers.append(pending.pop())
 
         def got(h, m, a, b, s=None):
             arrived(buf.at[spot(h, a, b), part(rows, h, s)], plane_sems, (t * 2 + h) * PLANE + m)
@@ -185,63 +191,71 @@
         yield 0
 
     class Reduce:
-        def __init__(self, buf, ra, rb, rc, rd, t, rows, finish, halves=(0, 1)):
+        def __init__(self, buf, ra, rb, rc, rd, t, cut, finish):
             self.buf, self.ra, self.rb, self.rc, self.rd = buf, ra, rb, rc, rd
-            self.t, self.rows, self.write, self.halves = t, rows, finish, halves
+            self.t, self.cut, self.write = t, cut, finish
+
+        def part(self, h, s=None):
+            return part(self.buf.shape[1], h, s, self.cut)
+
+        def land(self, ref, h, s, *index):
+            return ref.at[h, *index, pl.ds(0, self.part(h, s).size)]
 
         def send(self, h, m, a, b, s, dst, primary, k):
-            src = self.buf.at[spot(h, a, b), part(self.rows, h, s)]
+            src = self.buf.at[spot(h, a, b), self.part(h, s)]
             start(src, dst, plane_sems, (self.t * 2 + h) * PLANE + m, along(ring(h, primary), k))
 
         def got(self, h, m, dst):
             arrived(dst, plane_sems, (self.t * 2 + h) * PLANE + m)
 
         def add(self, h, a, b, s, *terms):
-            j, rows = spot(h, a, b), part(self.rows, h, s)
+            j, rows = spot(h, a, b), self.part(h, s)
             total = self.buf[j, rows].astype(F32)
             for term in terms:
-                total = total + term.astype(F32)
+                total = total + term[...].astype(F32)
             self.buf[j, rows] = total.astype(BF16)
 
-        def begin(self, *ks):
-            for k in ks:
-                for h in self.halves:
-                    self.send(h, 4 + 4 * k, k, 2, 0, self.ra.at[h, k, 0], False, 1)
-                    self.send(h, 5 + 4 * k, k, 2, 1, self.ra.at[h, k, 1], False, -1)
-
-        def middle(self, *ks):
-            for k in ks:
-                for h in self.halves:
+        def begin(self, k):
+            for h in (0, 1):
+                for s, way in ((0, 1), (1, -1)):
+                    self.send(h, 4 + 4 * k + s, k, 2, s, self.land(self.ra, h, s, k, s), False, way)
+
+        def middle(self, k):
+            for h in (0, 1):
+                for s, way in ((0, 1), (1, -1)):
+                    term = self.land(self.ra, h, s, k, s)
+                    self.got(h, 4 + 4 * k + s, term)
+                    self.add(h, k, way, s, term)
+                    self.send(h, 6 + 4 * k + s, k, way, None, self.land(self.rb, h, None, k, s), False, way)
+
+        def close(self, k):
+            for h in (0, 1):
+                terms = [self.land(self.rb, h, None, k, s) for s in (0, 1)]
+                for s in (0, 1):
+                    self.got(h, 6 + 4 * k + s, terms[s])
+                self.add(h, k, 0, None, *terms)
+                if k == 2:
                     for s, way in ((0, 1), (1, -1)):
-                        self.got(h, 4 + 4 * k + s, self.ra.at[h, k, s])
-                        self.add(h, k, way, s, self.ra[h, k, s])
-                        self.send(h, 6 + 4 * k + s, k, way, None, self.rb.at[h, k, s], False, way)
-
-        def close(self, *ks):
-            for k in ks:
-                for h in self.halves:
-                    for s in (0, 1):
-                        self.got(h, 6 + 4 * k + s, self.rb.at[h, k, s])
-                    self.add(h, k, 0, None, self.rb[h, k, 0], self.rb[h, k, 1])
-                    if k == 2:
-                        self.send(h, 0, 2, 0, 0, self.rc.at[h, 0], True, 1)
-                        self.send(h, 1, 2, 0, 1, self.rc.at[h, 1], True, -1)
+                        self.send(h, s, 2, 0, s, self.land(self.rc, h, s, s), True, way)
 
         def cross(self):
-            for h in self.halves:
+            for h in (0, 1):
                 for s, way in ((0, 1), (1, -1)):
-                    self.got(h, s, self.rc.at[h, s])
-                    self.add(h, way, 0, s, self.rc[h, s])
-                    self.send(h, 2 + s, way, 0, None, self.rd.at[h, s], True, way)
+                    term = self.land(self.rc, h, s, s)
+                    self.got(h, s, term)
+                    self.add(h, way, 0, s, term)
+                    self.send(h, 2 + s, way, 0, None, self.land(self.rd, h, None, s), True, way)
 
         def finish(self):
-            for h in self.halves:
+            for h in (0, 1):
+                terms = [self.land(self.rb, h, None, 0, s) for s in (0, 1)]
+                terms += [self.land(self.rd, h, None, s) for s in (0, 1)]
                 for s in (0, 1):
-                    self.got(h, 6 + s, self.rb.at[h, 0, s])
-                    self.got(h, 2 + s, self.rd.at[h, s])
-                total = self.buf[spot(h, 0, 0), part(self.rows, h)].astype(F32)
-                for term in (self.rb[h, 0, 0], self.rb[h, 0, 1], self.rd[h, 0], self.rd[h, 1]):
-                    total = total + term.astype(F32)
+                    self.got(h, 6 + s, terms[s])
+                    self.got(h, 2 + s, terms[2 + s])
+                total = self.buf[spot(h, 0, 0), self.part(h)].astype(F32)
+                for term in terms:
+                    total = total + term[...].astype(F32)
                 self.write(h, total)
 
     class HeadReduce:
@@ -298,26 +312,127 @@
             body(shard(*offsets(i)))
 
     own = shard(0, 0)
-    loads = []
-    for n, (src, dst) in enumerate(((hidden, hid), (d_out, dout))):
-        for j in range(SHARDS):
-            copy = pltpu.make_async_copy(src.at[:, pl.ds(j * ROWS, ROWS)], dst.at[j], load_sem.at[n * SHARDS + j])
-            copy.start()
-            loads.append(copy)
     barrier = pltpu.get_barrier_semaphore()
     others = [along("x", k) for k in (1, 2, 3)] + [along("y", k) for k in (1, 2, 3)]
     head_others = [device(h=lax.rem(head + k, 8)) for k in range(1, 8)]
     for target in others + head_others:
         pl.semaphore_signal(barrier, inc=1, device_id=target, device_id_type=MESH)
-    wg[own, :, 0:QC] = wq[...]
-    wg[own, :, QC:QC + HEAD_DIM] = wk[...]
-    wg[own, :, QC + HEAD_DIM:] = wv[...]
-    wog[own] = wo[...]
+    weights = [
+        (wq, wg.at[own, :, pl.ds(0, QC)]),
+        (wk, wg.at[own, :, pl.ds(QC, HEAD_DIM)]),
+        (wv, wg.at[own, :, pl.ds(QC + HEAD_DIM, HEAD_DIM)]),
+        (wo, wog.at[own]),
+    ]
+    rows = [(hidden.at[:, pl.ds(j * ROWS, ROWS)], hid.at[j]) for j in range(SHARDS)]
+    rows += [(d_out.at[:, pl.ds(j * ROWS, ROWS)], dout.at[j]) for j in range(SHARDS)]
+    loads = [pltpu.make_async_copy(src, dst, load_sem.at[n]) for n, (src, dst) in enumerate(rows + weights)]
+    for copy in loads[2 * SHARDS:]:
+        copy.start()
+    for copy in loads[2 * SHARDS:]:
+        copy.wait()
     pl.semaphore_wait(barrier, 13)
+
+    stores = []
+
+    def store(n, src, dst):
+        copy = pltpu.make_async_copy(src, dst, store_sem.at[n])
+        copy.start()
+        stores.append(copy)
 
     w_gather = gather(wg, 0, ROWS)
     o_gather = gather(wog, 1, QC)
     next(w_gather)
+    for copy in loads[:2 * SHARDS]:
+        copy.start()
+
+    def rotate(u):
+        return u * cosf[...] + pltpu.roll(u, HEAD_DIM // 2, 1) * sinf[...]
+
+    def unrotate(u):
+        return u * cosf[...] - pltpu.roll(u, HEAD_DIM // 2, 1) * sinf[...]
+
+    mine = pl.ds(pl.multiple_of(pair * HALF, HALF), HALF)
+    theirs = pl.ds(pl.multiple_of((1 - pair) * HALF, HALF), HALF)
+    partner = device(py=(y // 2) * 2 + 1 - pair)
+
+    def project(j):
+        pacc[...] += dot_nn(normed[j], wg[j])
+
+    def grad_attend(j):
+        gacc[...] += dot_nt(dout[j], wog[j])
+
+    def branch_terms(k):
+        first = 4 * step(z, k)
+
+        @pl.loop(0, 4)
+        def _(i):
+            hid[first + i] = dot_nn(att[...], wog[first + i]).astype(BF16)
+        branch_sum.swap(k)
+
+    def norm_terms(k):
+        first = 4 * step(z, k)
+
+        @pl.loop(0, 4)
+        def _(i):
+            normed[first + i] = dot_nt(dproj[...], wg[first + i]).astype(BF16)
+        norm_sum.swap(k)
+
+    def out_term(j):
+        go[j] = dot_nn(att_t[...], dout[j]).astype(BF16)
+
+    def query_term(j):
+        for h in range(2):
+            wog[j, h * ROWS:(h + 1) * ROWS] = dot_nn(norm_t[j], dproj[:, h * ROWS:(h + 1) * ROWS]).astype(BF16)
+
+    def kv_term(j):
+        gkv[j] = dot_nn(norm_t[j], dproj[:, QC:]).astype(BF16)
+
+    def out_finish(h, total):
+        g_wo[h * ROWS:(h + 1) * ROWS, :] = total
+        if h == 1:
+            store(5, g_wo, g_wo_out)
+
+    def query_finish(h, total):
+        g_wq[:, h * ROWS:(h + 1) * ROWS] = total
+        if h == 1:
+            store(2, g_wq, g_wq_out)
+
+    def kv_finish(h, total):
+        rows = slice(0, KV_CUT) if h == 0 else slice(KV_CUT, ROWS)
+        g_wk[rows, :] = total[:, :HEAD_DIM]
+        g_wv[rows, :] = total[:, HEAD_DIM:]
+        if h == 1:
+            store(3, g_wk, g_wk_out)
+            store(4, g_wv, g_wv_out)
+
+    out = Reduce(go, oa, ob, oc, od, 3, ROWS, out_finish)
+    query = Reduce(wog, qa, qb, qc, qd, 2, ROWS, query_finish)
+    kv = Reduce(gkv, va, vb, vc, vd, 4, KV_CUT, kv_finish)
+    branch_sum = HeadReduce(hid, p_core, p_za, p_zb, 0)
+    norm_sum = HeadReduce(normed, n_core, n_za, n_zb, 1)
+
+    def forward(g):
+        cols = slice(g * HEAD_DIM, (g + 1) * HEAD_DIM)
+        scores = dot_nt(qh[g], kall[...]) * SCALE + bias[...].astype(F32)
+        expo = jnp.exp(scores - jnp.max(scores, -1, keepdims=True))
+        prob = expo / jnp.sum(expo, -1, keepdims=True)
+        probs[g] = prob
+        attended = dot_nn(prob.astype(BF16), vall[...])
+        attf[:, cols] = attended
+        rounded = attended.astype(BF16)
+        att[:, cols] = rounded
+        att_t[cols, :] = rounded.T
+
+    def backward(g):
+        cols = slice(g * HEAD_DIM, (g + 1) * HEAD_DIM)
+        g_head = gatt[:, cols]
+        prob = probs[g]
+        d_prob = dot_nt(g_head, vall[...])
+        delta = jnp.sum(g_head.astype(F32) * attf[:, cols], -1, keepdims=True)
+        d_score = (prob * (d_prob - delta) * SCALE).astype(BF16)
+        dproj[:, cols] = unrotate(dot_nn(d_score, kall[...])).astype(BF16)
+        dkv[0] += dot_tn(d_score, qh[g])
+        dkv[1] += dot_tn(prob.astype(BF16), g_head)
 
     for copy in loads[:SHARDS]:
         copy.wait()
@@ -341,7 +456,15 @@
         norm_block(j)
     for i in range(2):
         hslice[i] = hid[2 * head + i]
-
+    next(w_gather)
+    pacc[...] = dot_nn(normed[own], wg[own])
+    next(w_gather)
+    next(w_gather)
+    next(w_gather)
+    each(3, project)
+    next(w_gather)
+    each(2, project)
+    each(4, project)
     prompt_length, resp_length = plen[0], rlen[0]
     slot = lax.broadcasted_iota(jnp.int32, (SLOTS, HEAD_DIM), 0)
     lane = lax.broadcasted_iota(jnp.int32, (8, HEAD_DIM), 1)
@@ -358,35 +481,11 @@
     resp_id = t_id - 2 * HALF
     resp_key = (t_id >= 2 * HALF) & (s_id >= HALF) & (resp_id <= s_id - HALF) & (resp_id < resp_length)
     bias[...] = jnp.where(prompt_key | resp_key, 0.0, -1e30).astype(BF16)
-
     next(w_gather)
-    pacc[...] = dot_nn(normed[own], wg[own])
-
-    def project(j):
-        pacc[...] += dot_nn(normed[j], wg[j])
-
-    def pump(gen, times=1, body=None):
-        for _ in range(times):
-            group = next(gen)
-            if group is not None and body is not None:
-                each(group, body)
-
-    early = []
-    for which in "wwwwwow":
-        if which == "w":
-            pump(w_gather, 1, project)
-        else:
-            early.append(next(o_gather))
-
-    def rotate(u):
-        return u * cosf[...] + pltpu.roll(u, HEAD_DIM // 2, 1) * sinf[...]
-
-    def unrotate(u):
-        return u * cosf[...] - pltpu.roll(u, HEAD_DIM // 2, 1) * sinf[...]
-
-    mine = pl.ds(pl.multiple_of(pair * HALF, HALF), HALF)
-    theirs = pl.ds(pl.multiple_of((1 - pair) * HALF, HALF), HALF)
-    partner = device(py=(y // 2) * 2 + 1 - pair)
+    next(o_gather)
+    next(w_gather)
+    each(1, project)
+    each(0, project)
     keys = rotate(pacc[:, QC:QC + HEAD_DIM]).astype(BF16)
     values = pacc[:, QC + HEAD_DIM:].astype(BF16)
     kall[mine] = keys[:HALF]
@@ -395,163 +494,103 @@
     vall[2 * HALF:] = values[HALF:]
     start(kall.at[mine], kall.at[mine], small_sems, 0, partner)
     start(vall.at[mine], vall.at[mine], small_sems, 1, partner)
+    next(o_gather)
+    for copy in loads[SHARDS:2 * SHARDS]:
+        copy.wait()
+    gacc[...] = dot_nt(dout[own], wog[own])
     for g in range(GROUP):
         qh[g] = rotate(pacc[:, g * HEAD_DIM:(g + 1) * HEAD_DIM]).astype(BF16)
-    for copy in loads[SHARDS:]:
-        copy.wait()
-    gacc = pacc.at[:, 0:QC]
-    gacc[...] = dot_nt(dout[own], wog[own])
-
-    def grad_attend(j):
-        gacc[...] += dot_nt(dout[j], wog[j])
-
-    def branch_term(j):
-        hid[j] = dot_nn(att[...], wog[j]).astype(BF16)
-
-    def out_term(j):
-        go[j] = dot_nn(att_t[...], dout[j]).astype(BF16)
-
-    for group in early:
-        if group is not None:
-            each(group, grad_attend)
-    pump(o_gather, 2, grad_attend)
+    next(o_gather)
+    each(4, grad_attend)
     arrived(kall.at[theirs], small_sems, 0)
     arrived(vall.at[theirs], small_sems, 1)
-
-    for g in range(GROUP):
-        cols = slice(g * HEAD_DIM, (g + 1) * HEAD_DIM)
-        scores = dot_nt(qh[g], kall[...]) * SCALE + bias[...].astype(F32)
-        expo = jnp.exp(scores - jnp.max(scores, -1, keepdims=True))
-        prob = expo / jnp.sum(expo, -1, keepdims=True)
-        probs[g] = prob
-        out = dot_nn(prob.astype(BF16), vall[...])
-        attf[:, cols] = out
-        rounded = out.astype(BF16)
-        att[:, cols] = rounded
-        att_t[cols, :] = rounded.T
-        pump(o_gather, (1, 1, 1, 1)[g], grad_attend)
-
-    def out_finish(h, total):
-        g_wo[h * ROWS:(h + 1) * ROWS, :] = total
-
-    out = Reduce(go, oa, ob, oc, od, 3, QC, out_finish)
-    branch_sum = HeadReduce(hid, p_core, p_za, p_zb, 0)
+    forward(0)
+    forward(1)
+    forward(2)
+    next(o_gather)
+    forward(3)
+    each(2, out_term)
+    each(1, out_term)
+    next(o_gather)
     each(0, out_term)
+    out.begin(3)
+    out.begin(0)
+    each(3, grad_attend)
+    next(o_gather)
+    each(2, grad_attend)
+    each(4, out_term)
+    each(3, out_term)
+    each(5, out_term)
+    next(o_gather)
     out.begin(2)
-    each(1, out_term)
-    out.begin(1, 3)
-    each(2, out_term)
-    out.begin(0)
-    each(3, out_term)
-    pump(o_gather, 1, grad_attend)
+    each(1, grad_attend)
+    out.begin(1)
+    out.middle(3)
+    out.middle(0)
+    next(o_gather)
+    each(0, grad_attend)
     gatt[...] = gacc[...].astype(BF16)
-    gather_sent = list(pending)
-    out.middle(2)
-
     dkv[...] = jnp.zeros_like(dkv)
-
-    def backward(g):
-        cols = slice(g * HEAD_DIM, (g + 1) * HEAD_DIM)
-        g_head = gatt[:, cols]
-        prob = probs[g]
-        d_prob = dot_nt(g_head, vall[...])
-        delta = jnp.sum(g_head.astype(F32) * attf[:, cols], -1, keepdims=True)
-        d_score = (prob * (d_prob - delta) * SCALE).astype(BF16)
-        dproj[:, cols] = unrotate(dot_nn(d_score, kall[...])).astype(BF16)
-        dkv[0] += dot_tn(d_score, qh[g])
-        dkv[1] += dot_tn(prob.astype(BF16), g_head)
-
     backward(0)
     backward(1)
-    each(4, out_term)
-    out.middle(1, 3)
     backward(2)
     backward(3)
     kv_out[0] = dkv[0, theirs].astype(BF16)
     kv_out[1] = dkv[1, theirs].astype(BF16)
     start(kv_out, kv_in, small_sems, 2, partner)
-    out.middle(0)
-    each(5, out_term)
-
-    @pl.loop(0, SHARDS)
-    def _(j):
-        branch_term(j)
-
-    for k in (2, 1, 3, 0):
-        branch_sum.swap(k)
-
-    for copy in gather_sent:
+    out.middle(2)
+    branch_terms(2)
+    out.middle(1)
+    branch_terms(3)
+    branch_terms(1)
+    for copy in gathers:
         copy.wait_send()
-        pending.remove(copy)
-
-    def query_term(j):
-        for h in range(2):
-            wog[j, h * ROWS:(h + 1) * ROWS] = dot_nn(norm_t[j], dproj[:, h * ROWS:(h + 1) * ROWS]).astype(BF16)
-
-    def kv_term(j):
-        gkv[j] = dot_nn(norm_t[j], dproj[:, QC:]).astype(BF16)
-
-    def query_finish(h, total):
-        g_wq[:, h * ROWS:(h + 1) * ROWS] = total
-
-    def kv_finish(h, total):
-        rows = slice(h * ROWS // 2, (h + 1) * ROWS // 2)
-        g_wk[rows, :] = total[:, :HEAD_DIM]
-        g_wv[rows, :] = total[:, HEAD_DIM:]
-
-    query = Reduce(wog, qa, qb, qc, qd, 2, QC, query_finish)
-    kv = Reduce(gkv, va, vb, vc, vd, 4, ROWS, kv_finish)
+    branch_terms(0)
     each(0, query_term)
     query.begin(2)
     each(1, query_term)
-    query.begin(1, 3)
+    query.begin(1)
     arrived(kv_in, small_sems, 2)
     d_keys = jnp.concatenate([dkv[0, mine] + kv_in[0].astype(F32), dkv[0, 2 * HALF:]], 0)
     d_values = jnp.concatenate([dkv[1, mine] + kv_in[1].astype(F32), dkv[1, 2 * HALF:]], 0)
     dproj[:, QC:QC + HEAD_DIM] = unrotate(d_keys).astype(BF16)
     dproj[:, QC + HEAD_DIM:] = d_values.astype(BF16)
-
-    norm_sum = HeadReduce(normed, n_core, n_za, n_zb, 1)
-
-    def norm_terms(k):
-        first = 4 * step(z, k)
-
-        @pl.loop(0, 4)
-        def _(i):
-            normed[first + i] = dot_nt(dproj[...], wg[first + i]).astype(BF16)
-        norm_sum.swap(k)
-
-    norm_terms(2)
-    norm_terms(1)
-    norm_terms(3)
-    norm_sum.begin()
-    out.close(2)
-    norm_terms(0)
-    each(2, query_term)
-    query.begin(0)
-    query.middle(2)
-    each(3, query_term)
-    query.middle(1, 3)
-    norm_sum.middle()
-    branch_sum.begin()
-    out.close(1, 3)
-    out.cross()
+    query.begin(3)
     each(0, kv_term)
     kv.begin(2)
     each(1, kv_term)
-    kv.begin(1, 3)
+    norm_terms(2)
+    branch_sum.begin()
+    out.close(2)
+    kv.begin(3)
+    norm_terms(1)
+    kv.begin(1)
+    each(2, query_term)
+    each(3, kv_term)
+    query.middle(2)
+    norm_terms(3)
+    query.begin(0)
+    out.close(1)
+    norm_sum.begin()
+    each(3, query_term)
+    query.middle(1)
+    out.close(3)
+    kv.middle(2)
+    each(2, kv_term)
+    each(5, query_term)
+    norm_sum.middle()
+    kv.begin(0)
+    query.close(2)
+    query.middle(3)
+    kv.middle(1)
+    norm_terms(0)
+    kv.close(2)
+    out.cross()
     each(4, query_term)
-    query.middle(0)
-    each(5, query_term)
-    query.close(2)
-    each(2, kv_term)
-    kv.begin(0)
-    each(3, kv_term)
-    kv.middle(2)
+    each(4, kv_term)
     branch_sum.middle()
-    out.finish()
+    kv.middle(3)
     shares = [norm_sum.total(i) for i in range(2)]
-
     row_part = jnp.zeros((SLOTS, HEAD_DIM), F32)
     for i in range(2):
         scaled = hslice[i].astype(F32) * inv[...]
@@ -567,18 +606,29 @@
         start(rstat.at[head], rstat.at[head], small_sems, 2 + k, head_others[k - 1])
     for k in range(1, 4):
         start(gx.at[x], gx.at[x], small_sems, 9 + k, along("x", k))
-    kv.middle(1, 3)
-    each(4, kv_term)
-    kv.middle(0)
-    each(5, kv_term)
+    query.middle(0)
+    kv.close(1)
+    query.close(1)
+    kv.close(3)
     for k in range(1, 4):
         arrived(gx.at[step(x, -k)], small_sems, 9 + k)
     gy[y] = jnp.sum(gx[...], 0)
     for k in range(1, 4):
         start(gy.at[y], gy.at[y], small_sems, 12 + k, along("y", k))
-    query.close(1, 3)
+    kv.cross()
+    query.close(3)
     query.cross()
-    kv.close(2)
+    kv.middle(0)
+    for i in range(2):
+        branch[:, i * ROWS:(i + 1) * ROWS] = branch_sum.total(i).astype(BF16)
+    store(0, branch, branch_out)
+    for k in range(1, 4):
+        arrived(gy.at[step(y, -k)], small_sems, 12 + k)
+    gh[head] = jnp.sum(gy[...], 0)
+    for k in range(1, 8):
+        start(gh.at[head], gh.at[head], small_sems, 15 + k, head_others[k - 1])
+    each(5, kv_term)
+    out.finish()
     for k in range(1, 8):
         arrived(rstat.at[lax.rem(head + 8 - k, 8)], small_sems, 2 + k)
     total = jnp.sum(rstat[...], 0)[0:1]
@@ -589,22 +639,17 @@
         factor = inv[:, half]
         scaled = hslice[i // 2, :, half].astype(F32) * factor
         g_hidden[:, cols] = factor * (g_hidden[:, cols] - scaled * mean)
-    for k in range(1, 4):
-        arrived(gy.at[step(y, -k)], small_sems, 12 + k)
-    gh[head] = jnp.sum(gy[...], 0)
-    for k in range(1, 8):
-        start(gh.at[head], gh.at[head], small_sems, 15 + k, head_others[k - 1])
-    for i in range(2):
-        branch[:, i * ROWS:(i + 1) * ROWS] = branch_sum.total(i).astype(BF16)
-    kv.close(1, 3)
-    kv.cross()
+    store(1, g_hidden, g_hidden_out)
     query.finish()
-    kv.finish()
     for k in range(1, 8):
         arrived(gh.at[lax.rem(head + 8 - k, 8)], small_sems, 15 + k)
     for i in range(8):
         g_gain[:, i * QC:(i + 1) * QC] = gh[i, 0:1, :]
+    store(6, g_gain, g_gain_out)
+    kv.finish()
     sent()
+    for copy in stores:
+        copy.wait()
 
 
 def place_kernel(*refs):
@@ -628,7 +673,17 @@
     smem = pl.BlockSpec(memory_space=pltpu.SMEM)
     anywhere = pl.BlockSpec(memory_space=pl.ANY)
     big = (SHARDS, SLOTS, ROWS)
-    scratch = [
+    results = (
+        jax.ShapeDtypeStruct((SLOTS, QC), BF16),
+        jax.ShapeDtypeStruct((SLOTS, QC), F32),
+        jax.ShapeDtypeStruct((ROWS, QC), F32),
+        jax.ShapeDtypeStruct((ROWS, HEAD_DIM), F32),
+        jax.ShapeDtypeStruct((ROWS, HEAD_DIM), F32),
+        jax.ShapeDtypeStruct((QC, ROWS), F32),
+        jax.ShapeDtypeStruct((1, 8 * QC), F32),
+    )
+    scratch = [pltpu.VMEM(out.shape, out.dtype) for out in results]
+    scratch += [
         pltpu.VMEM((SHARDS, ROWS, WC), BF16),
         pltpu.VMEM((SHARDS, QC, ROWS), BF16),
         pltpu.VMEM(big, BF16),
@@ -638,12 +693,13 @@
         pltpu.VMEM((SHARDS, QC, ROWS), BF16),
         pltpu.VMEM((SHARDS, ROWS, ROWS), BF16),
     ]
-    for rows, cols in ((QC, ROWS), (QC, ROWS), (ROWS, ROWS)):
+    for rows, cols, cut in ((QC, ROWS, QC // 2), (QC, ROWS, QC // 2), (ROWS, ROWS, KV_CUT)):
+        most = max(cut, rows - cut)
         scratch += [
-            pltpu.VMEM((2, 4, 2, rows // 4, cols), BF16),
-            pltpu.VMEM((2, 4, 2, rows // 2, cols), BF16),
-            pltpu.VMEM((2, 2, rows // 4, cols), BF16),
-            pltpu.VMEM((2, 2, rows // 2, cols), BF16),
+            pltpu.VMEM((2, 4, 2, most // 2, cols), BF16),
+            pltpu.VMEM((2, 4, 2, most, cols), BF16),
+            pltpu.VMEM((2, 2, most // 2, cols), BF16),
+            pltpu.VMEM((2, 2, most, cols), BF16),
         ]
     for _ in range(2):
         scratch += [
@@ -655,6 +711,7 @@
         pltpu.VMEM((GROUP, SLOTS, KEYS), F32),
         pltpu.VMEM((SLOTS, KEYS), BF16),
         pltpu.VMEM((SLOTS, WC), F32),
+        pltpu.VMEM((SLOTS, QC), F32),
         pltpu.VMEM((SLOTS, QC), F32),
         pltpu.VMEM((SLOTS, QC), BF16),
         pltpu.VMEM((QC, SLOTS), BF16),
@@ -674,7 +731,8 @@
         pltpu.VMEM((4, 8, QC), F32),
         pltpu.VMEM((4, 8, QC), F32),
         pltpu.VMEM((8, 8, QC), F32),
-        pltpu.SemaphoreType.DMA((2 * SHARDS,)),
+        pltpu.SemaphoreType.DMA((2 * SHARDS + 4,)),
+        pltpu.SemaphoreType.DMA((7,)),
         pltpu.SemaphoreType.DMA((10 * PLANE,)),
         pltpu.SemaphoreType.DMA((10 * PLANE,)),
         pltpu.SemaphoreType.DMA((24,)),
@@ -684,17 +742,9 @@
     ]
     outs = pl.pallas_call(
         kernel,
-        out_shape=(
-            jax.ShapeDtypeStruct((SLOTS, QC), BF16),
-            jax.ShapeDtypeStruct((SLOTS, QC), F32),
-            jax.ShapeDtypeStruct((ROWS, QC), F32),
-            jax.ShapeDtypeStruct((ROWS, HEAD_DIM), F32),
-            jax.ShapeDtypeStruct((ROWS, HEAD_DIM), F32),
-            jax.ShapeDtypeStruct((QC, ROWS), F32),
-            jax.ShapeDtypeStruct((1, 8 * QC), F32),
-        ),
-        in_specs=[anywhere, anywhere, vmem, vmem, vmem, vmem, vmem, smem, smem],
-        out_specs=(vmem,) * 7,
+        out_shape=results,
+        in_specs=[anywhere, anywhere, vmem, anywhere, anywhere, anywhere, anywhere, smem, smem],
+        out_specs=(anywhere,) * 7,
         scratch_shapes=scratch,
         compiler_params=pltpu.CompilerParams(
             collective_id=0, has_side_effects=True, vmem_limit_bytes=65011712

time: 139 us -> 133 us (0.957)
  Pallas kernels: 137 us -> 131 us
    pallas_call x1, Pallas kernels: 134 us -> 128 us  [shards(): pl.pallas_call(kernel, out_shape=results, in_specs=[anywhere, anywhere, v...]
where the time goes in v3:
time: 133 us
  Pallas kernels  131 us (98%)
  between operations  2.1 us (2%)
    pallas_call x1, Pallas kernels, shards(): pl.pallas_call(kernel, out_shape=results, in_specs=[anywhere, anywhere, v...  128 us
    pallas_call x1, Pallas kernels, shards(): pl.pallas_call(place_kernel, out_shape=tuple((jax.ShapeDtypeStruct(out.sh...  2.69 us

profile of v3, /device:TPU:1, one launch (start us, length us, event | category | flops | bytes accessed | tf_op | source)
XLA Modules:
  0.0 132.8 jit_solution(12147786485022403504)
XLA Ops:
  1.9 128.0 %attention_step.1 = (bf16[384,512]{1,0:T(8,128)(2,1)}, f32[384,512]{1,0:T(8,128)}, f32[256,512]{1,0:T(8,128)}, f32[256,128]{1,0:T(8,128)}, f32[256,128]{1,0:T(8,...) custom-call(bf16[384,4096]{1,0:T(8,128)(2,1)} %bitcast.8, bf16[384,4096]{1,0:T(8,128)(2,1)} %bitcast.9, ...), custom_call_target="tpu_custom_call" | custom-call | tf_op jit(solution)/shard_map/attention_step/pallas_call | solution.py:743
  129.9 2.7 %place_results.1 = (bf16[384,512]{1,0:T(8,128)(2,1)}, f32[384,512]{1,0:T(8,128)}, f32[256,512]{1,0:T(8,128)}, f32[256,128]{1,0:T(8,128)}, f32[256,128]{1,0:T(8,1...) custom-call(bf16[384,512]{1,0:T(8,128)(2,1)} %get-tuple-element.21.refs_0_, f32[384,512]{1,0:T(8,128)} %get-tuple-element.22.refs_1_, ...), custom_call_target="tpu_custom_call" | custom-call | tf_op jit(solution)/shard_map/place_results/pallas_call | solution.py:757

commit v4 on v3

--- a/solution.py
+++ b/solution.py
@@ -24,6 +24,7 @@
 F32 = jnp.float32
 BF16 = jnp.bfloat16
 PLANE = 20
+WINDOW = 48
 KV_CUT = 64
 
 
@@ -39,24 +40,20 @@
     return lax.dot_general(a, b, (((0,), (0,)), ((), ())), preferred_element_type=F32)
 
 
-def step(value, offset):
-    return lax.rem(value + offset % 4, 4)
-
-
 GROUPS = (
     (1, lambda i: (2, 2)),
-    (4, lambda i: ((1 + 2 * lax.rem(i, 2)) * (1 - i // 2) + 2 * (i // 2), 2 * (1 - i // 2) + (1 + 2 * lax.rem(i, 2)) * (i // 2))),
+    (4, lambda i: ((1 + 2 * lax.rem(i, 2)) * (1 - lax.div(i, 2)) + 2 * (lax.div(i, 2)), 2 * (1 - lax.div(i, 2)) + (1 + 2 * lax.rem(i, 2)) * (lax.div(i, 2)))),
     (2, lambda i: (2 * i, 2 * (1 - i))),
-    (4, lambda i: (1 + 2 * lax.rem(i, 2), 1 + 2 * (i // 2))),
-    (4, lambda i: ((1 + 2 * lax.rem(i, 2)) * (1 - i // 2), (1 + 2 * lax.rem(i, 2)) * (i // 2))),
+    (4, lambda i: (1 + 2 * lax.rem(i, 2), 1 + 2 * (lax.div(i, 2)))),
+    (4, lambda i: ((1 + 2 * lax.rem(i, 2)) * (1 - lax.div(i, 2)), (1 + 2 * lax.rem(i, 2)) * (lax.div(i, 2)))),
     (1, lambda i: (0, 0)),
 )
 
 
 def kernel(
-    hidden, d_out, gain, wq, wk, wv, wo, plen, rlen,
+    hidden, d_out, gain_in, wq, wk, wv, wo, plen, rlen,
     branch_out, g_hidden_out, g_wq_out, g_wk_out, g_wv_out, g_wo_out, g_gain_out,
-    branch, g_hidden, g_wq, g_wk, g_wv, g_wo, g_gain,
+    branch, g_hidden, g_wq, g_wk, g_wv, g_wo, g_gain, gain,
     wg, wog, hid, dout, normed, norm_t, go, gkv,
     oa, ob, oc, od, qa, qb, qc, qd, va, vb, vc, vd,
     p_core, p_za, p_zb, n_core, n_za, n_zb,
@@ -65,26 +62,34 @@
     load_sem, store_sem, send_sem, recv_sem, core_send, core_recv, small_send, small_recv,
 ):
     dp, head, pair = lax.axis_index("dp"), lax.axis_index("head"), lax.axis_index("pair")
-    x, y = lax.rem(dp, 4), (dp // 4) * 2 + pair
-    z, c = head // 2, lax.rem(head, 2)
+    x, y = lax.rem(dp, 4), lax.div(dp, 4) * 2 + pair
+    z, c = lax.div(head, 2), lax.rem(head, 2)
+
+    xs = [lax.rem(x + k, 4) for k in range(4)]
+    ys = [lax.rem(y + k, 4) for k in range(4)]
+    zs = [lax.rem(z + k, 4) for k in range(4)]
+    highs = [lax.div(v, 2) * 8 for v in ys]
+    lows = [lax.rem(v, 2) for v in ys]
+    shards_at = {(a, b): highs[b] + xs[a] * 2 + lows[b] for a in range(4) for b in range(4)}
 
     def place(px, py):
-        return ((py // 2) * 4 + px) * 2 + lax.rem(py, 2)
+        return (lax.div(py, 2) * 4 + px) * 2 + lax.rem(py, 2)
 
     def shard(dx, dy):
+        if isinstance(dx, int) and isinstance(dy, int):
+            return shards_at[dx % 4, dy % 4]
         return place(lax.rem(x + dx, 4), lax.rem(y + dy, 4))
 
-    def device(px=x, py=y, h=head):
-        return ((py // 2) * 4 + px, h, lax.rem(py, 2))
+    blocks = {(k, same): zs[k] * 4 + 2 * (c if same else 1 - c) for k in range(4) for same in (0, 1)}
+    dps = [lax.div(v, 2) * 4 + x for v in ys]
+    targets = {("x", k): (dps[0] - x + xs[k], head, pair) for k in range(1, 4)}
+    targets.update({("y", k): (dps[k], head, lows[k]) for k in range(1, 4)})
+    targets.update({("z", k): (dp, zs[k] * 2 + c, pair) for k in range(1, 4)})
+    targets["core", 1] = (dp, z * 2 + (1 - c), pair)
+    heads = [lax.rem(head + k, 8) for k in range(8)]
 
     def along(axis, k):
-        if axis == "x":
-            return device(px=step(x, k))
-        if axis == "y":
-            return device(py=step(y, k))
-        if axis == "z":
-            return device(h=step(z, k) * 2 + c)
-        return device(h=z * 2 + (1 - c))
+        return targets[axis, k % 4]
 
     pending, gathers = [], []
 
@@ -100,6 +105,8 @@
         )
         copy.start()
         pending.append(copy)
+        if len(pending) > WINDOW:
+            pending.pop(0).wait_send()
         return copy
 
     def arrived(dst, sems, index):
@@ -130,6 +137,8 @@
             ref = buf.at[spot(h, a, b), part(rows, h, s)]
             start(ref, ref, plane_sems, (t * 2 + h) * PLANE + m, along(ring(h, primary), k))
             gathers.append(pending.pop())
+            if len(gathers) > WINDOW:
+                gathers.pop(0).wait_send()
 
         def got(h, m, a, b, s=None):
             arrived(buf.at[spot(h, a, b), part(rows, h, s)], plane_sems, (t * 2 + h) * PLANE + m)
@@ -215,83 +224,76 @@
                 total = total + term[...].astype(F32)
             self.buf[j, rows] = total.astype(BF16)
 
-        def begin(self, k):
-            for h in (0, 1):
+        def begin(self, k, h):
+            for s, way in ((0, 1), (1, -1)):
+                self.send(h, 4 + 4 * k + s, k, 2, s, self.land(self.ra, h, s, k, s), False, way)
+
+        def middle(self, k, h):
+            for s, way in ((0, 1), (1, -1)):
+                term = self.land(self.ra, h, s, k, s)
+                self.got(h, 4 + 4 * k + s, term)
+                self.add(h, k, way, s, term)
+                self.send(h, 6 + 4 * k + s, k, way, None, self.land(self.rb, h, None, k, s), False, way)
+
+        def close(self, k, h):
+            terms = [self.land(self.rb, h, None, k, s) for s in (0, 1)]
+            for s in (0, 1):
+                self.got(h, 6 + 4 * k + s, terms[s])
+            self.add(h, k, 0, None, *terms)
+            if k == 2:
                 for s, way in ((0, 1), (1, -1)):
-                    self.send(h, 4 + 4 * k + s, k, 2, s, self.land(self.ra, h, s, k, s), False, way)
-
-        def middle(self, k):
-            for h in (0, 1):
-                for s, way in ((0, 1), (1, -1)):
-                    term = self.land(self.ra, h, s, k, s)
-                    self.got(h, 4 + 4 * k + s, term)
-                    self.add(h, k, way, s, term)
-                    self.send(h, 6 + 4 * k + s, k, way, None, self.land(self.rb, h, None, k, s), False, way)
-
-        def close(self, k):
-            for h in (0, 1):
-                terms = [self.land(self.rb, h, None, k, s) for s in (0, 1)]
-                for s in (0, 1):
-                    self.got(h, 6 + 4 * k + s, terms[s])
-                self.add(h, k, 0, None, *terms)
-                if k == 2:
-                    for s, way in ((0, 1), (1, -1)):
-                        self.send(h, s, 2, 0, s, self.land(self.rc, h, s, s), True, way)
-
-        def cross(self):
-            for h in (0, 1):
-                for s, way in ((0, 1), (1, -1)):
-                    term = self.land(self.rc, h, s, s)
-                    self.got(h, s, term)
-                    self.add(h, way, 0, s, term)
-                    self.send(h, 2 + s, way, 0, None, self.land(self.rd, h, None, s), True, way)
-
-        def finish(self):
-            for h in (0, 1):
-                terms = [self.land(self.rb, h, None, 0, s) for s in (0, 1)]
-                terms += [self.land(self.rd, h, None, s) for s in (0, 1)]
-                for s in (0, 1):
-                    self.got(h, 6 + s, terms[s])
-                    self.got(h, 2 + s, terms[2 + s])
-                total = self.buf[spot(h, 0, 0), self.part(h)].astype(F32)
-                for term in terms:
-                    total = total + term[...].astype(F32)
-                self.write(h, total)
+                    self.send(h, s, 2, 0, s, self.land(self.rc, h, s, s), True, way)
+
+        def cross(self, h):
+            for s, way in ((0, 1), (1, -1)):
+                term = self.land(self.rc, h, s, s)
+                self.got(h, s, term)
+                self.add(h, way, 0, s, term)
+                self.send(h, 2 + s, way, 0, None, self.land(self.rd, h, None, s), True, way)
+
+        def finish(self, h):
+            terms = [self.land(self.rb, h, None, 0, s) for s in (0, 1)]
+            terms += [self.land(self.rd, h, None, s) for s in (0, 1)]
+            for s in (0, 1):
+                self.got(h, 6 + s, terms[s])
+                self.got(h, 2 + s, terms[2 + s])
+            total = self.buf[spot(h, 0, 0), self.part(h)].astype(F32)
+            for term in terms:
+                total = total + term[...].astype(F32)
+            self.write(h, total)
 
     class HeadReduce:
         def __init__(self, buf, r_core, r_za, r_zb, t):
             self.buf, self.r_core, self.r_za, self.r_zb, self.base = buf, r_core, r_za, r_zb, t * 12
 
-        def block(self, k, core):
-            return 2 * (step(z, k) * 2 + core)
+        def block(self, k, same):
+            return blocks[k % 4, same]
 
         def add(self, k, i, rows, term):
-            j = self.block(k, c) + i
+            j = self.block(k, 1) + i
             self.buf[j, rows] = (self.buf[j, rows].astype(F32) + term.astype(F32)).astype(BF16)
 
         def swap(self, k):
-            start(self.buf.at[pl.ds(self.block(k, 1 - c), 2)], self.r_core.at[k], core_sems, self.base + k, along("core", 1))
-
-        def begin(self):
-            arrived(self.r_core.at[2], core_sems, self.base + 2)
-            for i in range(2):
-                self.add(2, i, pl.ds(0, SLOTS), self.r_core[2, i])
-                for s, way in ((0, 1), (1, -1)):
-                    rows = pl.ds(s * SLOTS // 2, SLOTS // 2)
-                    src = self.buf.at[self.block(2, c) + i, rows]
-                    start(src, self.r_za.at[s, i], core_sems, self.base + 4 + 2 * s + i, along("z", way))
-
-        def middle(self):
-            for way in (1, -1):
-                arrived(self.r_core.at[way % 4], core_sems, self.base + way % 4)
-                for i in range(2):
-                    self.add(way, i, pl.ds(0, SLOTS), self.r_core[way % 4, i])
-            for i in range(2):
-                for s, way in ((0, 1), (1, -1)):
-                    arrived(self.r_za.at[s, i], core_sems, self.base + 4 + 2 * s + i)
-                    self.add(way, i, pl.ds(s * SLOTS // 2, SLOTS // 2), self.r_za[s, i])
-                    src = self.buf.at[self.block(way, c) + i]
-                    start(src, self.r_zb.at[s, i], core_sems, self.base + 8 + 2 * s + i, along("z", way))
+            start(self.buf.at[pl.ds(self.block(k, 0), 2)], self.r_core.at[k], core_sems, self.base + k, along("core", 1))
+
+        def begin(self, i):
+            if i == 0:
+                arrived(self.r_core.at[2], core_sems, self.base + 2)
+            self.add(2, i, pl.ds(0, SLOTS), self.r_core[2, i])
+            for s, way in ((0, 1), (1, -1)):
+                rows = pl.ds(s * SLOTS // 2, SLOTS // 2)
+                src = self.buf.at[self.block(2, 1) + i, rows]
+                start(src, self.r_za.at[s, i], core_sems, self.base + 4 + 2 * s + i, along("z", way))
+
+        def middle(self, i):
+            for s, way in ((0, 1), (1, -1)):
+                if i == 0:
+                    arrived(self.r_core.at[way % 4], core_sems, self.base + way % 4)
+                self.add(way, i, pl.ds(0, SLOTS), self.r_core[way % 4, i])
+                arrived(self.r_za.at[s, i], core_sems, self.base + 4 + 2 * s + i)
+                self.add(way, i, pl.ds(s * SLOTS // 2, SLOTS // 2), self.r_za[s, i])
+                src = self.buf.at[self.block(way, 1) + i]
+                start(src, self.r_zb.at[s, i], core_sems, self.base + 8 + 2 * s + i, along("z", way))
 
         def total(self, i):
             if i == 0:
@@ -314,7 +316,7 @@
     own = shard(0, 0)
     barrier = pltpu.get_barrier_semaphore()
     others = [along("x", k) for k in (1, 2, 3)] + [along("y", k) for k in (1, 2, 3)]
-    head_others = [device(h=lax.rem(head + k, 8)) for k in range(1, 8)]
+    head_others = [(dp, heads[k], pair) for k in range(1, 8)]
     for target in others + head_others:
         pl.semaphore_signal(barrier, inc=1, device_id=target, device_id_type=MESH)
     weights = [
@@ -322,6 +324,7 @@
         (wk, wg.at[own, :, pl.ds(QC, HEAD_DIM)]),
         (wv, wg.at[own, :, pl.ds(QC + HEAD_DIM, HEAD_DIM)]),
         (wo, wog.at[own]),
+        (gain_in, gain),
     ]
     rows = [(hidden.at[:, pl.ds(j * ROWS, ROWS)], hid.at[j]) for j in range(SHARDS)]
     rows += [(d_out.at[:, pl.ds(j * ROWS, ROWS)], dout.at[j]) for j in range(SHARDS)]
@@ -353,7 +356,7 @@
 
     mine = pl.ds(pl.multiple_of(pair * HALF, HALF), HALF)
     theirs = pl.ds(pl.multiple_of((1 - pair) * HALF, HALF), HALF)
-    partner = device(py=(y // 2) * 2 + 1 - pair)
+    partner = (dp, head, 1 - pair)
 
     def project(j):
         pacc[...] += dot_nn(normed[j], wg[j])
@@ -361,49 +364,51 @@
     def grad_attend(j):
         gacc[...] += dot_nt(dout[j], wog[j])
 
-    def branch_terms(k):
-        first = 4 * step(z, k)
-
-        @pl.loop(0, 4)
-        def _(i):
-            hid[first + i] = dot_nn(att[...], wog[first + i]).astype(BF16)
-        branch_sum.swap(k)
+    def branch_term(j):
+        hid[j] = dot_nn(att[...], wog[j]).astype(BF16)
 
     def norm_terms(k):
-        first = 4 * step(z, k)
+        first = 4 * zs[k]
 
         @pl.loop(0, 4)
         def _(i):
             normed[first + i] = dot_nt(dproj[...], wg[first + i]).astype(BF16)
         norm_sum.swap(k)
 
-    def out_term(j):
-        go[j] = dot_nn(att_t[...], dout[j]).astype(BF16)
-
-    def query_term(j):
-        for h in range(2):
-            wog[j, h * ROWS:(h + 1) * ROWS] = dot_nn(norm_t[j], dproj[:, h * ROWS:(h + 1) * ROWS]).astype(BF16)
+    def out_term(h):
+        rows = slice(h * ROWS, (h + 1) * ROWS)
+
+        def term(j):
+            go[j, rows] = dot_nn(att_t[rows], dout[j]).astype(BF16)
+
+        return term
+
+    def query_term(h):
+        cols = slice(h * ROWS, (h + 1) * ROWS)
+
+        def term(j):
+            wog[j, cols] = dot_nn(norm_t[j], dproj[:, cols]).astype(BF16)
+
+        return term
 
     def kv_term(j):
         gkv[j] = dot_nn(norm_t[j], dproj[:, QC:]).astype(BF16)
 
     def out_finish(h, total):
         g_wo[h * ROWS:(h + 1) * ROWS, :] = total
-        if h == 1:
-            store(5, g_wo, g_wo_out)
+        store(5 + 2 * h, g_wo.at[pl.ds(h * ROWS, ROWS)], g_wo_out.at[pl.ds(h * ROWS, ROWS)])
 
     def query_finish(h, total):
         g_wq[:, h * ROWS:(h + 1) * ROWS] = total
-        if h == 1:
-            store(2, g_wq, g_wq_out)
+        store(2 + 6 * h, g_wq.at[:, pl.ds(h * ROWS, ROWS)], g_wq_out.at[:, pl.ds(h * ROWS, ROWS)])
 
     def kv_finish(h, total):
         rows = slice(0, KV_CUT) if h == 0 else slice(KV_CUT, ROWS)
         g_wk[rows, :] = total[:, :HEAD_DIM]
         g_wv[rows, :] = total[:, HEAD_DIM:]
-        if h == 1:
-            store(3, g_wk, g_wk_out)
-            store(4, g_wv, g_wv_out)
+        piece = pl.ds(0, KV_CUT) if h == 0 else pl.ds(KV_CUT, ROWS - KV_CUT)
+        store(3 + 6 * h, g_wk.at[piece], g_wk_out.at[piece])
+        store(4 + 6 * h, g_wv.at[piece], g_wv_out.at[piece])
 
     out = Reduce(go, oa, ob, oc, od, 3, ROWS, out_finish)
     query = Reduce(wog, qa, qb, qc, qd, 2, ROWS, query_finish)
@@ -456,15 +461,17 @@
         norm_block(j)
     for i in range(2):
         hslice[i] = hid[2 * head + i]
-    next(w_gather)
     pacc[...] = dot_nn(normed[own], wg[own])
+    for copy in loads[SHARDS:2 * SHARDS]:
+        copy.wait()
+    gacc[...] = dot_nt(dout[own], wog[own])
     next(w_gather)
     next(w_gather)
     next(w_gather)
+    next(w_gather)
+    each(4, project)
+    next(w_gather)
     each(3, project)
-    next(w_gather)
-    each(2, project)
-    each(4, project)
     prompt_length, resp_length = plen[0], rlen[0]
     slot = lax.broadcasted_iota(jnp.int32, (SLOTS, HEAD_DIM), 0)
     lane = lax.broadcasted_iota(jnp.int32, (8, HEAD_DIM), 1)
@@ -483,9 +490,10 @@
     bias[...] = jnp.where(prompt_key | resp_key, 0.0, -1e30).astype(BF16)
     next(w_gather)
     next(o_gather)
+    each(2, project)
     next(w_gather)
+    each(0, project)
     each(1, project)
-    each(0, project)
     keys = rotate(pacc[:, QC:QC + HEAD_DIM]).astype(BF16)
     values = pacc[:, QC + HEAD_DIM:].astype(BF16)
     kall[mine] = keys[:HALF]
@@ -495,9 +503,6 @@
     start(kall.at[mine], kall.at[mine], small_sems, 0, partner)
     start(vall.at[mine], vall.at[mine], small_sems, 1, partner)
     next(o_gather)
-    for copy in loads[SHARDS:2 * SHARDS]:
-        copy.wait()
-    gacc[...] = dot_nt(dout[own], wog[own])
     for g in range(GROUP):
         qh[g] = rotate(pacc[:, g * HEAD_DIM:(g + 1) * HEAD_DIM]).astype(BF16)
     next(o_gather)
@@ -507,89 +512,137 @@
     forward(0)
     forward(1)
     forward(2)
+    forward(3)
+    each(0, out_term(1))
+    each(5, branch_term)
     next(o_gather)
-    forward(3)
-    each(2, out_term)
-    each(1, out_term)
+    each(1, out_term(1))
+    each(4, branch_term)
+    out.begin(1, 1)
+    each(0, out_term(0))
+    out.begin(2, 1)
     next(o_gather)
-    each(0, out_term)
-    out.begin(3)
-    out.begin(0)
     each(3, grad_attend)
+    each(2, out_term(1))
+    out.begin(3, 1)
     next(o_gather)
+    each(2, branch_term)
+    each(2, out_term(0))
     each(2, grad_attend)
-    each(4, out_term)
-    each(3, out_term)
-    each(5, out_term)
+    each(3, out_term(1))
+    out.begin(2, 0)
+    each(3, branch_term)
     next(o_gather)
-    out.begin(2)
+    out.middle(1, 1)
     each(1, grad_attend)
-    out.begin(1)
-    out.middle(3)
-    out.middle(0)
+    out.begin(0, 0)
+    each(1, out_term(0))
     next(o_gather)
+    out.begin(3, 0)
+    out.middle(2, 1)
+    out.middle(2, 0)
     each(0, grad_attend)
     gatt[...] = gacc[...].astype(BF16)
+    out.middle(3, 1)
+    for copy in gathers:
+        copy.wait_send()
+    each(1, branch_term)
+    each(0, branch_term)
     dkv[...] = jnp.zeros_like(dkv)
     backward(0)
+    out.begin(1, 0)
     backward(1)
     backward(2)
+    branch_sum.swap(3)
+    out.begin(0, 1)
+    branch_sum.swap(2)
+    branch_sum.swap(1)
+    branch_sum.swap(0)
+    each(0, query_term(0))
+    query.begin(2, 0)
     backward(3)
+    each(1, query_term(1))
     kv_out[0] = dkv[0, theirs].astype(BF16)
     kv_out[1] = dkv[1, theirs].astype(BF16)
     start(kv_out, kv_in, small_sems, 2, partner)
-    out.middle(2)
-    branch_terms(2)
-    out.middle(1)
-    branch_terms(3)
-    branch_terms(1)
-    for copy in gathers:
-        copy.wait_send()
-    branch_terms(0)
-    each(0, query_term)
-    query.begin(2)
-    each(1, query_term)
-    query.begin(1)
+    each(1, query_term(0))
+    out.close(2, 0)
+    query.begin(3, 1)
+    out.close(2, 1)
+    each(4, out_term(1))
+    each(0, query_term(1))
+    query.begin(2, 1)
+    each(2, query_term(1))
+    query.middle(2, 0)
+    each(3, out_term(0))
+    out.middle(0, 1)
+    out.middle(1, 0)
+    query.begin(3, 0)
+    each(2, query_term(0))
     arrived(kv_in, small_sems, 2)
     d_keys = jnp.concatenate([dkv[0, mine] + kv_in[0].astype(F32), dkv[0, 2 * HALF:]], 0)
     d_values = jnp.concatenate([dkv[1, mine] + kv_in[1].astype(F32), dkv[1, 2 * HALF:]], 0)
     dproj[:, QC:QC + HEAD_DIM] = unrotate(d_keys).astype(BF16)
     dproj[:, QC + HEAD_DIM:] = d_values.astype(BF16)
-    query.begin(3)
+    query.begin(1, 1)
+    each(1, kv_term)
+    kv.begin(3, 0)
+    each(5, query_term(1))
+    each(3, query_term(0))
+    norm_terms(2)
+    query.begin(0, 1)
+    query.middle(2, 1)
+    norm_terms(1)
+    kv.begin(1, 1)
+    query.begin(1, 0)
     each(0, kv_term)
-    kv.begin(2)
-    each(1, kv_term)
-    norm_terms(2)
-    branch_sum.begin()
-    out.close(2)
-    kv.begin(3)
-    norm_terms(1)
-    kv.begin(1)
-    each(2, query_term)
+    query.begin(0, 0)
+    out.close(3, 1)
+    kv.begin(2, 1)
+    kv.begin(1, 0)
+    norm_sum.begin(0)
+    norm_terms(3)
+    each(3, query_term(1))
+    norm_sum.begin(1)
+    kv.begin(2, 0)
+    out.middle(3, 0)
+    query.middle(1, 1)
+    each(4, query_term(0))
+    norm_sum.middle(0)
+    kv.begin(3, 1)
+    query.middle(1, 0)
+    query.middle(3, 1)
+    branch_sum.begin(0)
     each(3, kv_term)
-    query.middle(2)
-    norm_terms(3)
-    query.begin(0)
-    out.close(1)
-    norm_sum.begin()
-    each(3, query_term)
-    query.middle(1)
-    out.close(3)
-    kv.middle(2)
     each(2, kv_term)
-    each(5, query_term)
-    norm_sum.middle()
-    kv.begin(0)
-    query.close(2)
-    query.middle(3)
-    kv.middle(1)
+    query.middle(3, 0)
+    query.close(2, 0)
+    kv.middle(1, 0)
     norm_terms(0)
-    kv.close(2)
-    out.cross()
-    each(4, query_term)
-    each(4, kv_term)
-    branch_sum.middle()
-    kv.middle(3)
+    norm_sum.middle(1)
+    each(5, kv_term)
+    out.close(1, 1)
+    each(4, out_term(0))
+    kv.middle(3, 1)
+    kv.middle(3, 0)
+    out.close(1, 0)
+    kv.middle(2, 0)
+    branch_sum.begin(1)
+    kv.begin(0, 1)
+    each(5, query_term(0))
+    out.cross(1)
+    kv.middle(2, 1)
+    out.middle(0, 0)
+    each(4, query_term(1))
+    out.close(3, 0)
+    kv.begin(0, 0)
+    each(5, out_term(1))
+    branch_sum.middle(0)
+    kv.close(2, 0)
+    out.cross(0)
+    query.middle(0, 0)
+    query.close(2, 1)
+    kv.middle(1, 1)
     shares = [norm_sum.total(i) for i in range(2)]
     row_part = jnp.zeros((SLOTS, HEAD_DIM), F32)
     for i in range(2):
@@ -606,47 +659,62 @@
         start(rstat.at[head], rstat.at[head], small_sems, 2 + k, head_others[k - 1])
     for k in range(1, 4):
         start(gx.at[x], gx.at[x], small_sems, 9 + k, along("x", k))
-    query.middle(0)
-    kv.close(1)
-    query.close(1)
-    kv.close(3)
+    query.close(3, 0)
+    query.middle(0, 1)
+    query.close(3, 1)
+    kv.close(2, 1)
+    query.close(1, 0)
+    each(4, kv_term)
+    query.cross(0)
+    query.close(1, 1)
+    kv.close(1, 0)
+    branch_sum.middle(1)
+    kv.middle(0, 0)
+    kv.close(3, 0)
+    kv.cross(0)
     for k in range(1, 4):
-        arrived(gx.at[step(x, -k)], small_sems, 9 + k)
+        arrived(gx.at[xs[-k % 4]], small_sems, 9 + k)
     gy[y] = jnp.sum(gx[...], 0)
     for k in range(1, 4):
         start(gy.at[y], gy.at[y], small_sems, 12 + k, along("y", k))
-    kv.cross()
-    query.close(3)
-    query.cross()
-    kv.middle(0)
-    for i in range(2):
-        branch[:, i * ROWS:(i + 1) * ROWS] = branch_sum.total(i).astype(BF16)
-    store(0, branch, branch_out)
-    for k in range(1, 4):
-        arrived(gy.at[step(y, -k)], small_sems, 12 + k)
-    gh[head] = jnp.sum(gy[...], 0)
+    kv.close(3, 1)
+    kv.close(1, 1)
+    query.cross(1)
     for k in range(1, 8):
-        start(gh.at[head], gh.at[head], small_sems, 15 + k, head_others[k - 1])
-    each(5, kv_term)
-    out.finish()
-    for k in range(1, 8):
-        arrived(rstat.at[lax.rem(head + 8 - k, 8)], small_sems, 2 + k)
+        arrived(rstat.at[heads[8 - k]], small_sems, 2 + k)
     total = jnp.sum(rstat[...], 0)[0:1]
     mean = jnp.broadcast_to(total, (HEAD_DIM, SLOTS)).T * (1.0 / (SHARDS * ROWS))
     for i in range(4):
         cols = slice(i * HEAD_DIM, (i + 1) * HEAD_DIM)
         half = slice((i % 2) * HEAD_DIM, (i % 2 + 1) * HEAD_DIM)
         factor = inv[:, half]
-        scaled = hslice[i // 2, :, half].astype(F32) * factor
+        scaled = hslice[lax.div(i, 2), :, half].astype(F32) * factor
         g_hidden[:, cols] = factor * (g_hidden[:, cols] - scaled * mean)
     store(1, g_hidden, g_hidden_out)
-    query.finish()
+    kv.cross(1)
+    kv.middle(0, 1)
+    for k in range(1, 4):
+        arrived(gy.at[ys[-k % 4]], small_sems, 12 + k)
+    gh[head] = jnp.sum(gy[...], 0)
     for k in range(1, 8):
-        arrived(gh.at[lax.rem(head + 8 - k, 8)], small_sems, 15 + k)
+        start(gh.at[head], gh.at[head], small_sems, 15 + k, head_others[k - 1])
+    each(5, out_term(0))
+    out.finish(0)
+    out.finish(1)
+    for i in range(2):
+        branch[:, i * ROWS:(i + 1) * ROWS] = branch_sum.total(i).astype(BF16)
+    store(0, branch, branch_out)
+    kv.finish(0)
+    query.finish(0)
+    query.finish(1)
+    for k in range(1, 8):
+        arrived(gh.at[heads[8 - k]], small_sems, 15 + k)
     for i in range(8):
         g_gain[:, i * QC:(i + 1) * QC] = gh[i, 0:1, :]
     store(6, g_gain, g_gain_out)
-    kv.finish()
+    while len(pending) > 24:
+        pending.pop(0).wait_send()
+    kv.finish(1)
     sent()
     for copy in stores:
         copy.wait()
@@ -669,7 +737,6 @@
 
 
 def shards(hidden, d_out, norm_gain, w_query, w_key, w_value, w_out, prompt_len, resp_len):
-    vmem = pl.BlockSpec(memory_space=pltpu.VMEM)
     smem = pl.BlockSpec(memory_space=pltpu.SMEM)
     anywhere = pl.BlockSpec(memory_space=pl.ANY)
     big = (SHARDS, SLOTS, ROWS)
@@ -684,6 +751,7 @@
     )
     scratch = [pltpu.VMEM(out.shape, out.dtype) for out in results]
     scratch += [
+        pltpu.VMEM((SHARDS, 1, ROWS), F32),
         pltpu.VMEM((SHARDS, ROWS, WC), BF16),
         pltpu.VMEM((SHARDS, QC, ROWS), BF16),
         pltpu.VMEM(big, BF16),
@@ -731,8 +799,8 @@
         pltpu.VMEM((4, 8, QC), F32),
         pltpu.VMEM((4, 8, QC), F32),
         pltpu.VMEM((8, 8, QC), F32),
-        pltpu.SemaphoreType.DMA((2 * SHARDS + 4,)),
-        pltpu.SemaphoreType.DMA((7,)),
+        pltpu.SemaphoreType.DMA((2 * SHARDS + 5,)),
+        pltpu.SemaphoreType.DMA((12,)),
         pltpu.SemaphoreType.DMA((10 * PLANE,)),
         pltpu.SemaphoreType.DMA((10 * PLANE,)),
         pltpu.SemaphoreType.DMA((24,)),
@@ -743,7 +811,7 @@
     outs = pl.pallas_call(
         kernel,
         out_shape=results,
-        in_specs=[anywhere, anywhere, vmem, anywhere, anywhere, anywhere, anywhere, smem, smem],
+        in_specs=[anywhere, anywhere, anywhere, anywhere, anywhere, anywhere, anywhere, smem, smem],
         out_specs=(anywhere,) * 7,
         scratch_shapes=scratch,
         compiler_params=pltpu.CompilerParams(

time: 133 us -> 131 us (0.985)
  Pallas kernels: 131 us -> 128 us
    pallas_call x1, Pallas kernels: 128 us -> 126 us  [shards(): pl.pallas_call(kernel, out_shape=results, in_specs=[anywhere, anywhere, a...]
where the time goes in v4:
time: 131 us
  Pallas kernels  128 us (98%)
  between operations  2.1 us (2%)
    pallas_call x1, Pallas kernels, shards(): pl.pallas_call(kernel, out_shape=results, in_specs=[anywhere, anywhere, a...  126 us
    pallas_call x1, Pallas kernels, shards(): pl.pallas_call(place_kernel, out_shape=tuple((jax.ShapeDtypeStruct(out.sh...  2.69 us

profile of v4, /device:TPU:1, one launch (start us, length us, event | category | flops | bytes accessed | tf_op | source)
XLA Modules:
  0.0 130.6 jit_solution(10368082104870553420)
XLA Ops:
  1.9 125.8 %attention_step.1 = (bf16[384,512]{1,0:T(8,128)(2,1)}, f32[384,512]{1,0:T(8,128)}, f32[256,512]{1,0:T(8,128)}, f32[256,128]{1,0:T(8,128)}, f32[256,128]{1,0:T(8,...) custom-call(bf16[384,4096]{1,0:T(8,128)(2,1)} %bitcast.8, bf16[384,4096]{1,0:T(8,128)(2,1)} %bitcast.9, ...), custom_call_target="tpu_custom_call" | custom-call | tf_op jit(solution)/shard_map/attention_step/pallas_call | solution.py:811
  127.7 2.7 %place_results.1 = (bf16[384,512]{1,0:T(8,128)(2,1)}, f32[384,512]{1,0:T(8,128)}, f32[256,512]{1,0:T(8,128)}, f32[256,128]{1,0:T(8,128)}, f32[256,128]{1,0:T(8,1...) custom-call(bf16[384,512]{1,0:T(8,128)(2,1)} %get-tuple-element.21.refs_0_, f32[384,512]{1,0:T(8,128)} %get-tuple-element.22.refs_1_, ...), custom_call_target="tpu_custom_call" | custom-call | tf_op jit(solution)/shard_map/place_results/pallas_call | solution.py:825

commit v5 on v4

--- a/solution.py
+++ b/solution.py
@@ -23,8 +23,7 @@
 MESH = pl.DeviceIdType.MESH
 F32 = jnp.float32
 BF16 = jnp.bfloat16
-PLANE = 20
-WINDOW = 48
+SLOT = 10
 KV_CUT = 64
 
 
@@ -91,33 +90,22 @@
     def along(axis, k):
         return targets[axis, k % 4]
 
-    pending, gathers = [], []
-
-    def sent():
-        for copy in pending:
-            copy.wait_send()
-        pending.clear()
-
-    def start(src, dst, sems, index, target):
-        copy = pltpu.make_async_remote_copy(
-            src_ref=src, dst_ref=dst, send_sem=sems[0].at[index], recv_sem=sems[1].at[index],
+    sems = {"plane": (send_sem, recv_sem), "core": (core_send, core_recv), "small": (small_send, small_recv)}
+
+    def remote(src, dst, kind, leave, land, target):
+        return pltpu.make_async_remote_copy(
+            src_ref=src, dst_ref=dst, send_sem=sems[kind][0].at[leave], recv_sem=sems[kind][1].at[land],
             device_id=target, device_id_type=MESH,
         )
-        copy.start()
-        pending.append(copy)
-        if len(pending) > WINDOW:
-            pending.pop(0).wait_send()
-        return copy
-
-    def arrived(dst, sems, index):
-        pltpu.make_async_remote_copy(
-            src_ref=dst, dst_ref=dst, send_sem=sems[0].at[index], recv_sem=sems[1].at[index],
-            device_id=along("x", 1), device_id_type=MESH,
-        ).wait_recv()
-
-    plane_sems = (send_sem, recv_sem)
-    core_sems = (core_send, core_recv)
-    small_sems = (small_send, small_recv)
+
+    def start(src, dst, kind, leave, land, target):
+        remote(src, dst, kind, leave, land, target).start()
+
+    def arrived(ref, kind, land):
+        remote(ref, ref, kind, 0, land, along("x", 1)).wait_recv()
+
+    def departed(ref, kind, leave):
+        remote(ref, ref, kind, leave, 0, along("x", 1)).wait_send()
 
     def spot(h, a, b):
         return shard(a % 4, b % 4) if h == 0 else shard(b % 4, a % 4)
@@ -133,70 +121,64 @@
         return pl.ds(first + s * count // 2, count // 2)
 
     def gather(buf, t, rows):
-        def go_(h, m, a, b, s, primary, k):
+        both = (0, 1)
+
+        def go_(h, slot, a, b, s, primary, k):
             ref = buf.at[spot(h, a, b), part(rows, h, s)]
-            start(ref, ref, plane_sems, (t * 2 + h) * PLANE + m, along(ring(h, primary), k))
-            gathers.append(pending.pop())
-            if len(gathers) > WINDOW:
-                gathers.pop(0).wait_send()
-
-        def got(h, m, a, b, s=None):
-            arrived(buf.at[spot(h, a, b), part(rows, h, s)], plane_sems, (t * 2 + h) * PLANE + m)
-
-        both = (0, 1)
-        for h in both:
-            go_(h, 0, 0, 0, None, True, 1)
-            go_(h, 1, 0, 0, None, True, -1)
-        for h in both:
-            go_(h, 4, 0, 0, None, False, 1)
-            go_(h, 5, 0, 0, None, False, -1)
+            start(ref, ref, "plane", t * 2 + h, (t * 2 + h) * SLOT + slot, along(ring(h, primary), k))
+
+        def pair(h, slot):
+            arrived(buf.at[pl.ds(0, 2), part(rows, h)], "plane", (t * 2 + h) * SLOT + slot)
+
+        def whole(h, slot, a, b):
+            arrived(buf.at[spot(h, a, b), part(rows, h)], "plane", (t * 2 + h) * SLOT + slot)
+
+        def pass_on(h, slot, a, b, primary):
+            for s, way in ((0, 1), (1, -1)):
+                place_a, place_b = (-way, b) if primary else (a, -way)
+                go_(h, slot, place_a, place_b, s, primary, way)
+
+        for h in both:
+            for way in (1, -1):
+                go_(h, 0, 0, 0, None, True, way)
+        for h in both:
+            for way in (1, -1):
+                go_(h, 2, 0, 0, None, False, way)
         yield
         for h in both:
-            got(h, 0, -1, 0)
-            go_(h, 2, -1, 0, 0, True, 1)
-            got(h, 1, 1, 0)
-            go_(h, 3, 1, 0, 1, True, -1)
+            pair(h, 0)
+            pass_on(h, 1, None, 0, True)
         for h in both:
             for k in (1, 3):
-                go_(h, 4 + 4 * k, k, 0, None, False, 1)
-                go_(h, 5 + 4 * k, k, 0, None, False, -1)
+                for way in (1, -1):
+                    go_(h, 2 + k, k, 0, None, False, way)
         yield
         for h in both:
-            got(h, 4, 0, -1)
-            go_(h, 6, 0, -1, 0, False, 1)
-            got(h, 5, 0, 1)
-            go_(h, 7, 0, 1, 1, False, -1)
+            pair(h, 2)
+            pass_on(h, 6, 0, None, False)
         yield 4
         for h in both:
-            got(h, 2, 2, 0, 0)
-            got(h, 3, 2, 0, 1)
-            go_(h, 12, 2, 0, None, False, 1)
-            go_(h, 13, 2, 0, None, False, -1)
+            whole(h, 1, 2, 0)
+            for way in (1, -1):
+                go_(h, 4, 2, 0, None, False, way)
         yield
         for k in (1, 3):
             for h in both:
-                got(h, 4 + 4 * k, k, -1)
-                go_(h, 6 + 4 * k, k, -1, 0, False, 1)
-                got(h, 5 + 4 * k, k, 1)
-                go_(h, 7 + 4 * k, k, 1, 1, False, -1)
+                pair(h, 2 + k)
+                pass_on(h, 6 + k, k, None, False)
         yield 3
         for h in both:
-            got(h, 6, 0, 2, 0)
-            got(h, 7, 0, 2, 1)
+            whole(h, 6, 0, 2)
         yield 2
         for h in both:
-            got(h, 12, 2, -1)
-            go_(h, 14, 2, -1, 0, False, 1)
-            got(h, 13, 2, 1)
-            go_(h, 15, 2, 1, 1, False, -1)
+            pair(h, 4)
+            pass_on(h, 8, 2, None, False)
         for h in both:
             for k in (1, 3):
-                got(h, 6 + 4 * k, k, 2, 0)
-                got(h, 7 + 4 * k, k, 2, 1)
+                whole(h, 6 + k, k, 2)
         yield 1
         for h in both:
-            got(h, 14, 2, 2, 0)
-            got(h, 15, 2, 2, 1)
+            whole(h, 8, 2, 2)
         yield 0
 
     class Reduce:
@@ -210,12 +192,12 @@
         def land(self, ref, h, s, *index):
             return ref.at[h, *index, pl.ds(0, self.part(h, s).size)]
 
-        def send(self, h, m, a, b, s, dst, primary, k):
+        def send(self, h, slot, a, b, s, dst, primary, k):
             src = self.buf.at[spot(h, a, b), self.part(h, s)]
-            start(src, dst, plane_sems, (self.t * 2 + h) * PLANE + m, along(ring(h, primary), k))
-
-        def got(self, h, m, dst):
-            arrived(dst, plane_sems, (self.t * 2 + h) * PLANE + m)
+            start(src, dst, "plane", self.t * 2 + h, (self.t * 2 + h) * SLOT + slot, along(ring(h, primary), k))
+
+        def got(self, h, slot, ref):
+            arrived(ref, "plane", (self.t * 2 + h) * SLOT + slot)
 
         def add(self, h, a, b, s, *terms):
             j, rows = spot(h, a, b), self.part(h, s)
@@ -226,37 +208,32 @@
 
         def begin(self, k, h):
             for s, way in ((0, 1), (1, -1)):
-                self.send(h, 4 + 4 * k + s, k, 2, s, self.land(self.ra, h, s, k, s), False, way)
+                self.send(h, k, k, 2, s, self.land(self.ra, h, s, k, s), False, way)
 
         def middle(self, k, h):
+            self.got(h, k, self.land(self.ra, h, 0, k, slice(None)))
             for s, way in ((0, 1), (1, -1)):
-                term = self.land(self.ra, h, s, k, s)
-                self.got(h, 4 + 4 * k + s, term)
-                self.add(h, k, way, s, term)
-                self.send(h, 6 + 4 * k + s, k, way, None, self.land(self.rb, h, None, k, s), False, way)
+                self.add(h, k, way, s, self.land(self.ra, h, s, k, s))
+                self.send(h, 4 + k, k, way, None, self.land(self.rb, h, None, k, s), False, way)
 
         def close(self, k, h):
-            terms = [self.land(self.rb, h, None, k, s) for s in (0, 1)]
-            for s in (0, 1):
-                self.got(h, 6 + 4 * k + s, terms[s])
-            self.add(h, k, 0, None, *terms)
+            self.got(h, 4 + k, self.land(self.rb, h, None, k, slice(None)))
+            self.add(h, k, 0, None, *[self.land(self.rb, h, None, k, s) for s in (0, 1)])
             if k == 2:
                 for s, way in ((0, 1), (1, -1)):
-                    self.send(h, s, 2, 0, s, self.land(self.rc, h, s, s), True, way)
+                    self.send(h, 8, 2, 0, s, self.land(self.rc, h, s, s), True, way)
 
         def cross(self, h):
+            self.got(h, 8, self.land(self.rc, h, 0, slice(None)))
             for s, way in ((0, 1), (1, -1)):
-                term = self.land(self.rc, h, s, s)
-                self.got(h, s, term)
-                self.add(h, way, 0, s, term)
-                self.send(h, 2 + s, way, 0, None, self.land(self.rd, h, None, s), True, way)
+                self.add(h, way, 0, s, self.land(self.rc, h, s, s))
+                self.send(h, 9, way, 0, None, self.land(self.rd, h, None, s), True, way)
 
         def finish(self, h):
+            self.got(h, 4, self.land(self.rb, h, None, 0, slice(None)))
+            self.got(h, 9, self.land(self.rd, h, None, slice(None)))
             terms = [self.land(self.rb, h, None, 0, s) for s in (0, 1)]
             terms += [self.land(self.rd, h, None, s) for s in (0, 1)]
-            for s in (0, 1):
-                self.got(h, 6 + s, terms[s])
-                self.got(h, 2 + s, terms[2 + s])
             total = self.buf[spot(h, 0, 0), self.part(h)].astype(F32)
             for term in terms:
                 total = total + term[...].astype(F32)
@@ -264,7 +241,7 @@
 
     class HeadReduce:
         def __init__(self, buf, r_core, r_za, r_zb, t):
-            self.buf, self.r_core, self.r_za, self.r_zb, self.base = buf, r_core, r_za, r_zb, t * 12
+            self.buf, self.r_core, self.r_za, self.r_zb, self.t = buf, r_core, r_za, r_zb, t
 
         def block(self, k, same):
             return blocks[k % 4, same]
@@ -274,34 +251,37 @@
             self.buf[j, rows] = (self.buf[j, rows].astype(F32) + term.astype(F32)).astype(BF16)
 
         def swap(self, k):
-            start(self.buf.at[pl.ds(self.block(k, 0), 2)], self.r_core.at[k], core_sems, self.base + k, along("core", 1))
+            start(self.buf.at[pl.ds(self.block(k, 0), 2)], self.r_core.at[k], "core", self.t, self.t * 8 + k, along("core", 1))
+
+        def got(self, slot, ref):
+            arrived(ref, "core", self.t * 8 + slot)
 
         def begin(self, i):
             if i == 0:
-                arrived(self.r_core.at[2], core_sems, self.base + 2)
+                self.got(2, self.r_core.at[2])
             self.add(2, i, pl.ds(0, SLOTS), self.r_core[2, i])
             for s, way in ((0, 1), (1, -1)):
                 rows = pl.ds(s * SLOTS // 2, SLOTS // 2)
                 src = self.buf.at[self.block(2, 1) + i, rows]
-                start(src, self.r_za.at[s, i], core_sems, self.base + 4 + 2 * s + i, along("z", way))
+                start(src, self.r_za.at[i, s], "core", self.t, self.t * 8 + 4 + i, along("z", way))
 
         def middle(self, i):
+            if i == 0:
+                self.got(1, self.r_core.at[1])
+                self.got(3, self.r_core.at[3])
+            self.got(4 + i, self.r_za.at[i])
             for s, way in ((0, 1), (1, -1)):
-                if i == 0:
-                    arrived(self.r_core.at[way % 4], core_sems, self.base + way % 4)
                 self.add(way, i, pl.ds(0, SLOTS), self.r_core[way % 4, i])
-                arrived(self.r_za.at[s, i], core_sems, self.base + 4 + 2 * s + i)
-                self.add(way, i, pl.ds(s * SLOTS // 2, SLOTS // 2), self.r_za[s, i])
+                self.add(way, i, pl.ds(s * SLOTS // 2, SLOTS // 2), self.r_za[i, s])
                 src = self.buf.at[self.block(way, 1) + i]
-                start(src, self.r_zb.at[s, i], core_sems, self.base + 8 + 2 * s + i, along("z", way))
+                start(src, self.r_zb.at[i, s], "core", self.t, self.t * 8 + 6 + i, along("z", way))
 
         def total(self, i):
             if i == 0:
-                arrived(self.r_core.at[0], core_sems, self.base)
-            for s in range(2):
-                arrived(self.r_zb.at[s, i], core_sems, self.base + 8 + 2 * s + i)
+                self.got(0, self.r_core.at[0])
+            self.got(6 + i, self.r_zb.at[i])
             own_term = self.buf[2 * head + i].astype(F32) + self.r_core[0, i].astype(F32)
-            return own_term + self.r_zb[0, i].astype(F32) + self.r_zb[1, i].astype(F32)
+            return own_term + self.r_zb[i, 0].astype(F32) + self.r_zb[i, 1].astype(F32)
 
     def each(group, body):
         count, offsets = GROUPS[group]
@@ -326,12 +306,10 @@
         (wo, wog.at[own]),
         (gain_in, gain),
     ]
-    rows = [(hidden.at[:, pl.ds(j * ROWS, ROWS)], hid.at[j]) for j in range(SHARDS)]
-    rows += [(d_out.at[:, pl.ds(j * ROWS, ROWS)], dout.at[j]) for j in range(SHARDS)]
-    loads = [pltpu.make_async_copy(src, dst, load_sem.at[n]) for n, (src, dst) in enumerate(rows + weights)]
-    for copy in loads[2 * SHARDS:]:
+    loads = [pltpu.make_async_copy(src, dst, load_sem.at[2 + n]) for n, (src, dst) in enumerate(weights)]
+    for copy in loads:
         copy.start()
-    for copy in loads[2 * SHARDS:]:
+    for copy in loads:
         copy.wait()
     pl.semaphore_wait(barrier, 13)
 
@@ -345,8 +323,9 @@
     w_gather = gather(wg, 0, ROWS)
     o_gather = gather(wog, 1, QC)
     next(w_gather)
-    for copy in loads[:2 * SHARDS]:
-        copy.start()
+    for n, (src, dst) in enumerate(((hidden, hid), (d_out, dout))):
+        for j in range(SHARDS):
+            pltpu.make_async_copy(src.at[:, pl.ds(j * ROWS, ROWS)], dst.at[j], load_sem.at[n]).start()
 
     def rotate(u):
         return u * cosf[...] + pltpu.roll(u, HEAD_DIM // 2, 1) * sinf[...]
@@ -439,8 +418,7 @@
         dkv[0] += dot_tn(d_score, qh[g])
         dkv[1] += dot_tn(prob.astype(BF16), g_head)
 
-    for copy in loads[:SHARDS]:
-        copy.wait()
+    pltpu.make_async_copy(hid, hid, load_sem.at[0]).wait()
     pacc[:, 0:ROWS] = jnp.zeros((SLOTS, ROWS), F32)
 
     @pl.loop(0, SHARDS)
@@ -462,16 +440,16 @@
     for i in range(2):
         hslice[i] = hid[2 * head + i]
     pacc[...] = dot_nn(normed[own], wg[own])
-    for copy in loads[SHARDS:2 * SHARDS]:
-        copy.wait()
-    gacc[...] = dot_nt(dout[own], wog[own])
-    next(w_gather)
     next(w_gather)
     next(w_gather)
     next(w_gather)
     each(4, project)
     next(w_gather)
     each(3, project)
+    next(w_gather)
+    next(w_gather)
+    next(o_gather)
+    each(1, project)
     prompt_length, resp_length = plen[0], rlen[0]
     slot = lax.broadcasted_iota(jnp.int32, (SLOTS, HEAD_DIM), 0)
     lane = lax.broadcasted_iota(jnp.int32, (8, HEAD_DIM), 1)
@@ -489,160 +467,164 @@
     resp_key = (t_id >= 2 * HALF) & (s_id >= HALF) & (resp_id <= s_id - HALF) & (resp_id < resp_length)
     bias[...] = jnp.where(prompt_key | resp_key, 0.0, -1e30).astype(BF16)
     next(w_gather)
-    next(o_gather)
     each(2, project)
-    next(w_gather)
     each(0, project)
-    each(1, project)
     keys = rotate(pacc[:, QC:QC + HEAD_DIM]).astype(BF16)
     values = pacc[:, QC + HEAD_DIM:].astype(BF16)
     kall[mine] = keys[:HALF]
     kall[2 * HALF:] = keys[HALF:]
     vall[mine] = values[:HALF]
     vall[2 * HALF:] = values[HALF:]
-    start(kall.at[mine], kall.at[mine], small_sems, 0, partner)
-    start(vall.at[mine], vall.at[mine], small_sems, 1, partner)
+    start(kall.at[mine], kall.at[mine], "small", 0, 0, partner)
+    start(vall.at[mine], vall.at[mine], "small", 6, 6, partner)
+    pltpu.make_async_copy(dout, dout, load_sem.at[1]).wait()
+    gacc[...] = dot_nt(dout[own], wog[own])
     next(o_gather)
     for g in range(GROUP):
         qh[g] = rotate(pacc[:, g * HEAD_DIM:(g + 1) * HEAD_DIM]).astype(BF16)
     next(o_gather)
     each(4, grad_attend)
-    arrived(kall.at[theirs], small_sems, 0)
-    arrived(vall.at[theirs], small_sems, 1)
+    arrived(kall.at[theirs], "small", 0)
+    arrived(vall.at[theirs], "small", 6)
     forward(0)
     forward(1)
     forward(2)
+    next(o_gather)
     forward(3)
+    each(0, out_term(0))
+    each(1, out_term(0))
+    each(2, out_term(0))
+    each(1, out_term(1))
+    each(3, out_term(0))
+    out.begin(1, 1)
+    each(2, out_term(1))
+    next(o_gather)
+    each(3, out_term(1))
+    out.begin(3, 0)
+    out.begin(3, 1)
+    each(3, grad_attend)
+    each(4, branch_term)
+    out.begin(1, 0)
+    out.begin(0, 1)
     each(0, out_term(1))
-    each(5, branch_term)
-    next(o_gather)
-    each(1, out_term(1))
-    each(4, branch_term)
-    out.begin(1, 1)
-    each(0, out_term(0))
     out.begin(2, 1)
     next(o_gather)
-    each(3, grad_attend)
-    each(2, out_term(1))
-    out.begin(3, 1)
+    each(3, branch_term)
+    each(2, grad_attend)
     next(o_gather)
+    out.middle(3, 1)
+    each(5, branch_term)
+    out.middle(3, 0)
     each(2, branch_term)
-    each(2, out_term(0))
-    each(2, grad_attend)
-    each(3, out_term(1))
+    out.middle(1, 1)
+    each(1, branch_term)
+    out.middle(2, 1)
+    next(o_gather)
+    each(0, branch_term)
+    branch_sum.swap(1)
+    out.middle(1, 0)
+    out.begin(0, 0)
     out.begin(2, 0)
-    each(3, branch_term)
-    next(o_gather)
-    out.middle(1, 1)
+    branch_sum.swap(3)
     each(1, grad_attend)
-    out.begin(0, 0)
-    each(1, out_term(0))
-    next(o_gather)
-    out.begin(3, 0)
-    out.middle(2, 1)
-    out.middle(2, 0)
+    for t, buf, rows in ((0, wg, ROWS), (1, wog, QC)):
+        for h in range(2):
+            departed(buf.at[pl.ds(0, 15), part(rows, h)], "plane", t * 2 + h)
     each(0, grad_attend)
+    branch_sum.swap(2)
+    branch_sum.swap(0)
     gatt[...] = gacc[...].astype(BF16)
-    out.middle(3, 1)
-    for copy in gathers:
-        copy.wait_send()
-    each(1, branch_term)
-    each(0, branch_term)
     dkv[...] = jnp.zeros_like(dkv)
     backward(0)
-    out.begin(1, 0)
     backward(1)
     backward(2)
-    branch_sum.swap(3)
-    out.begin(0, 1)
-    branch_sum.swap(2)
-    branch_sum.swap(1)
-    branch_sum.swap(0)
-    each(0, query_term(0))
-    query.begin(2, 0)
     backward(3)
     each(1, query_term(1))
     kv_out[0] = dkv[0, theirs].astype(BF16)
     kv_out[1] = dkv[1, theirs].astype(BF16)
-    start(kv_out, kv_in, small_sems, 2, partner)
+    start(kv_out, kv_in, "small", 1, 1, partner)
+    query.begin(3, 1)
+    query.begin(1, 1)
+    each(0, query_term(1))
     each(1, query_term(0))
-    out.close(2, 0)
-    query.begin(3, 1)
-    out.close(2, 1)
-    each(4, out_term(1))
-    each(0, query_term(1))
+    each(2, query_term(0))
+    each(3, query_term(1))
     query.begin(2, 1)
+    query.begin(3, 0)
+    each(3, query_term(0))
+    each(4, out_term(0))
     each(2, query_term(1))
-    query.middle(2, 0)
-    each(3, out_term(0))
-    out.middle(0, 1)
-    out.middle(1, 0)
-    query.begin(3, 0)
-    each(2, query_term(0))
-    arrived(kv_in, small_sems, 2)
+    query.begin(0, 1)
+    out.middle(0, 0)
+    out.middle(2, 0)
+    query.begin(1, 0)
+    query.middle(1, 1)
+    arrived(kv_in, "small", 1)
     d_keys = jnp.concatenate([dkv[0, mine] + kv_in[0].astype(F32), dkv[0, 2 * HALF:]], 0)
     d_values = jnp.concatenate([dkv[1, mine] + kv_in[1].astype(F32), dkv[1, 2 * HALF:]], 0)
     dproj[:, QC:QC + HEAD_DIM] = unrotate(d_keys).astype(BF16)
     dproj[:, QC + HEAD_DIM:] = d_values.astype(BF16)
-    query.begin(1, 1)
+    norm_terms(2)
     each(1, kv_term)
+    query.middle(3, 1)
+    query.middle(3, 0)
+    each(2, kv_term)
+    kv.begin(1, 1)
+    each(4, out_term(1))
+    out.close(3, 0)
+    kv.begin(1, 0)
+    branch_sum.begin(0)
+    kv.begin(3, 1)
+    out.middle(0, 1)
+    norm_terms(3)
+    branch_sum.begin(1)
+    kv.begin(0, 0)
+    each(0, query_term(0))
     kv.begin(3, 0)
-    each(5, query_term(1))
-    each(3, query_term(0))
-    norm_terms(2)
-    query.begin(0, 1)
+    each(5, kv_term)
+    norm_sum.begin(0)
+    each(5, out_term(1))
+    out.close(2, 0)
     query.middle(2, 1)
+    each(0, kv_term)
+    kv.begin(2, 0)
     norm_terms(1)
-    kv.begin(1, 1)
-    query.begin(1, 0)
-    each(0, kv_term)
+    kv.begin(2, 1)
+    each(5, query_term(0))
     query.begin(0, 0)
+    each(4, query_term(0))
+    each(4, kv_term)
+    out.close(1, 0)
+    query.begin(2, 0)
     out.close(3, 1)
-    kv.begin(2, 1)
-    kv.begin(1, 0)
-    norm_sum.begin(0)
-    norm_terms(3)
-    each(3, query_term(1))
+    query.middle(1, 0)
     norm_sum.begin(1)
-    kv.begin(2, 0)
-    out.middle(3, 0)
-    query.middle(1, 1)
-    each(4, query_term(0))
+    each(3, kv_term)
+    out.close(2, 1)
     norm_sum.middle(0)
-    kv.begin(3, 1)
-    query.middle(1, 0)
-    query.middle(3, 1)
-    branch_sum.begin(0)
-    each(3, kv_term)
-    each(2, kv_term)
-    query.middle(3, 0)
+    kv.begin(0, 1)
+    out.cross(0)
+    kv.middle(2, 0)
+    norm_terms(0)
+    kv.middle(3, 1)
+    norm_sum.middle(1)
+    query.middle(2, 0)
+    each(4, query_term(1))
+    query.close(2, 1)
+    branch_sum.middle(0)
+    query.close(1, 0)
+    query.close(3, 0)
+    kv.middle(2, 1)
+    query.close(1, 1)
+    query.middle(0, 0)
+    kv.middle(1, 0)
     query.close(2, 0)
-    kv.middle(1, 0)
-    norm_terms(0)
-    norm_sum.middle(1)
-    each(5, kv_term)
+    each(5, out_term(0))
     out.close(1, 1)
-    each(4, out_term(0))
-    kv.middle(3, 1)
+    kv.middle(1, 1)
     kv.middle(3, 0)
-    out.close(1, 0)
-    kv.middle(2, 0)
-    branch_sum.begin(1)
-    kv.begin(0, 1)
-    each(5, query_term(0))
+    kv.close(2, 0)
     out.cross(1)
-    kv.middle(2, 1)
-    out.middle(0, 0)
-    each(4, query_term(1))
-    out.close(3, 0)
-    kv.begin(0, 0)
-    each(5, out_term(1))
-    branch_sum.middle(0)
-    kv.close(2, 0)
-    out.cross(0)
-    query.middle(0, 0)
-    query.close(2, 1)
-    kv.middle(1, 1)
     shares = [norm_sum.total(i) for i in range(2)]
     row_part = jnp.zeros((SLOTS, HEAD_DIM), F32)
     for i in range(2):
@@ -656,32 +638,36 @@
     row_sum = jnp.sum(row_part.T, 0, keepdims=True)
     rstat[head] = jnp.broadcast_to(row_sum, (8, SLOTS))
     for k in range(1, 8):
-        start(rstat.at[head], rstat.at[head], small_sems, 2 + k, head_others[k - 1])
+        start(rstat.at[head], rstat.at[head], "small", 2, 2, head_others[k - 1])
     for k in range(1, 4):
-        start(gx.at[x], gx.at[x], small_sems, 9 + k, along("x", k))
-    query.close(3, 0)
-    query.middle(0, 1)
+        start(gx.at[x], gx.at[x], "small", 3, 3, along("x", k))
+    query.cross(0)
     query.close(3, 1)
     kv.close(2, 1)
-    query.close(1, 0)
-    each(4, kv_term)
-    query.cross(0)
-    query.close(1, 1)
+    branch_sum.middle(1)
+    kv.close(3, 0)
+    query.middle(0, 1)
     kv.close(1, 0)
-    branch_sum.middle(1)
-    kv.middle(0, 0)
-    kv.close(3, 0)
-    kv.cross(0)
-    for k in range(1, 4):
-        arrived(gx.at[xs[-k % 4]], small_sems, 9 + k)
+    arrived(gx.at[pl.ds(0, 3)], "small", 3)
     gy[y] = jnp.sum(gx[...], 0)
     for k in range(1, 4):
-        start(gy.at[y], gy.at[y], small_sems, 12 + k, along("y", k))
+        start(gy.at[y], gy.at[y], "small", 4, 4, along("y", k))
+    query.cross(1)
+    kv.close(1, 1)
+    kv.middle(0, 0)
     kv.close(3, 1)
-    kv.close(1, 1)
-    query.cross(1)
+    out.finish(0)
+    kv.cross(0)
+    arrived(gy.at[pl.ds(0, 3)], "small", 4)
+    gh[head] = jnp.sum(gy[...], 0)
     for k in range(1, 8):
-        arrived(rstat.at[heads[8 - k]], small_sems, 2 + k)
+        start(gh.at[head], gh.at[head], "small", 5, 5, head_others[k - 1])
+    query.finish(0)
+    kv.cross(1)
+    kv.middle(0, 1)
+    each(5, query_term(1))
+    out.finish(1)
+    arrived(rstat.at[pl.ds(0, 7)], "small", 2)
     total = jnp.sum(rstat[...], 0)[0:1]
     mean = jnp.broadcast_to(total, (HEAD_DIM, SLOTS)).T * (1.0 / (SHARDS * ROWS))
     for i in range(4):
@@ -691,31 +677,24 @@
         scaled = hslice[lax.div(i, 2), :, half].astype(F32) * factor
         g_hidden[:, cols] = factor * (g_hidden[:, cols] - scaled * mean)
     store(1, g_hidden, g_hidden_out)
-    kv.cross(1)
-    kv.middle(0, 1)
-    for k in range(1, 4):
-        arrived(gy.at[ys[-k % 4]], small_sems, 12 + k)
-    gh[head] = jnp.sum(gy[...], 0)
-    for k in range(1, 8):
-        start(gh.at[head], gh.at[head], small_sems, 15 + k, head_others[k - 1])
-    each(5, out_term(0))
-    out.finish(0)
-    out.finish(1)
+    kv.finish(0)
     for i in range(2):
         branch[:, i * ROWS:(i + 1) * ROWS] = branch_sum.total(i).astype(BF16)
     store(0, branch, branch_out)
-    kv.finish(0)
-    query.finish(0)
     query.finish(1)
-    for k in range(1, 8):
-        arrived(gh.at[heads[8 - k]], small_sems, 15 + k)
+    kv.finish(1)
+    arrived(gh.at[pl.ds(0, 7)], "small", 5)
     for i in range(8):
         g_gain[:, i * QC:(i + 1) * QC] = gh[i, 0:1, :]
     store(6, g_gain, g_gain_out)
-    while len(pending) > 24:
-        pending.pop(0).wait_send()
-    kv.finish(1)
-    sent()
+    for reduction in (out, query, kv):
+        for h in range(2):
+            departed(reduction.buf.at[pl.ds(0, 15), reduction.part(h)], "plane", reduction.t * 2 + h)
+    for n, buf in enumerate((hid, normed)):
+        departed(buf.at[pl.ds(0, 14)], "core", n)
+    small = (kall.at[mine], kv_out, rstat.at[pl.ds(0, 7)], gx.at[pl.ds(0, 3)], gy.at[pl.ds(0, 3)], gh.at[pl.ds(0, 7)], vall.at[mine])
+    for n, ref in enumerate(small):
+        departed(ref, "small", n)
     for copy in stores:
         copy.wait()
 
@@ -799,14 +778,14 @@
         pltpu.VMEM((4, 8, QC), F32),
         pltpu.VMEM((4, 8, QC), F32),
         pltpu.VMEM((8, 8, QC), F32),
-        pltpu.SemaphoreType.DMA((2 * SHARDS + 5,)),
-        pltpu.SemaphoreType.DMA((12,)),
-        pltpu.SemaphoreType.DMA((10 * PLANE,)),
-        pltpu.SemaphoreType.DMA((10 * PLANE,)),
-        pltpu.SemaphoreType.DMA((24,)),
-        pltpu.SemaphoreType.DMA((24,)),
-        pltpu.SemaphoreType.DMA((24,)),
-        pltpu.SemaphoreType.DMA((24,)),
+        pltpu.SemaphoreType.DMA((7,)),
+        pltpu.SemaphoreType.DMA((11,)),
+        pltpu.SemaphoreType.DMA((10,)),
+        pltpu.SemaphoreType.DMA((10 * SLOT,)),
+        pltpu.SemaphoreType.DMA((2,)),
+        pltpu.SemaphoreType.DMA((16,)),
+        pltpu.SemaphoreType.DMA((7,)),
+        pltpu.SemaphoreType.DMA((7,)),
     ]
     outs = pl.pallas_call(
         kernel,

time: 131 us -> 129 us (0.985)
    pallas_call x1, Pallas kernels: 126 us -> 124 us  [shards(): pl.pallas_call(kernel, out_shape=results, in_specs=[anywhere, anywhere, a...]
where the time goes in v5:
time: 129 us
  Pallas kernels  127 us (98%)
  between operations  2.1 us (2%)
    pallas_call x1, Pallas kernels, shards(): pl.pallas_call(kernel, out_shape=results, in_specs=[anywhere, anywhere, a...  124 us
    pallas_call x1, Pallas kernels, shards(): pl.pallas_call(place_kernel, out_shape=tuple((jax.ShapeDtypeStruct(out.sh...  2.69 us

profile of v5, /device:TPU:1, one launch (start us, length us, event | category | flops | bytes accessed | tf_op | source)
XLA Modules:
  0.0 128.7 jit_solution(1757500649561378675)
XLA Ops:
  1.9 123.9 %attention_step.1 = (bf16[384,512]{1,0:T(8,128)(2,1)}, f32[384,512]{1,0:T(8,128)}, f32[256,512]{1,0:T(8,128)}, f32[256,128]{1,0:T(8,128)}, f32[256,128]{1,0:T(8,...) custom-call(bf16[384,4096]{1,0:T(8,128)(2,1)} %bitcast.8, bf16[384,4096]{1,0:T(8,128)(2,1)} %bitcast.9, ...), custom_call_target="tpu_custom_call" | custom-call | tf_op jit(solution)/shard_map/attention_step/pallas_call | solution.py:790
  125.8 2.7 %place_results.1 = (bf16[384,512]{1,0:T(8,128)(2,1)}, f32[384,512]{1,0:T(8,128)}, f32[256,512]{1,0:T(8,128)}, f32[256,128]{1,0:T(8,128)}, f32[256,128]{1,0:T(8,1...) custom-call(bf16[384,512]{1,0:T(8,128)(2,1)} %get-tuple-element.21.refs_0_, f32[384,512]{1,0:T(8,128)} %get-tuple-element.22.refs_1_, ...), custom_call_target="tpu_custom_call" | custom-call | tf_op jit(solution)/shard_map/place_results/pallas_call | solution.py:804

commit v6 on v5

--- a/solution.py
+++ b/solution.py
@@ -289,7 +289,7 @@
             body(shard(*offsets(0)))
             return
 
-        @pl.loop(0, count)
+        @pl.loop(0, count, unroll=2)
         def _(i):
             body(shard(*offsets(i)))
 
@@ -349,7 +349,7 @@
     def norm_terms(k):
         first = 4 * zs[k]
 
-        @pl.loop(0, 4)
+        @pl.loop(0, 4, unroll=2)
         def _(i):
             normed[first + i] = dot_nt(dproj[...], wg[first + i]).astype(BF16)
         norm_sum.swap(k)

time: 129 us -> 128 us (level)
  no operation moved by 1% of the time
where the time goes in v6:
time: 128 us
  Pallas kernels  126 us (98%)
  between operations  2.1 us (2%)
    pallas_call x1, Pallas kernels, shards(): pl.pallas_call(kernel, out_shape=results, in_specs=[anywhere, anywhere, a...  123 us
    pallas_call x1, Pallas kernels, shards(): pl.pallas_call(place_kernel, out_shape=tuple((jax.ShapeDtypeStruct(out.sh...  2.69 us

profile of v6, /device:TPU:1, one launch (start us, length us, event | category | flops | bytes accessed | tf_op | source)
XLA Modules:
  0.0 128.1 jit_solution(4174192738781544139)
XLA Ops:
  1.9 123.3 %attention_step.1 = (bf16[384,512]{1,0:T(8,128)(2,1)}, f32[384,512]{1,0:T(8,128)}, f32[256,512]{1,0:T(8,128)}, f32[256,128]{1,0:T(8,128)}, f32[256,128]{1,0:T(8,...) custom-call(bf16[384,4096]{1,0:T(8,128)(2,1)} %bitcast.8, bf16[384,4096]{1,0:T(8,128)(2,1)} %bitcast.9, ...), custom_call_target="tpu_custom_call" | custom-call | tf_op jit(solution)/shard_map/attention_step/pallas_call | solution.py:790
  125.2 2.7 %place_results.1 = (bf16[384,512]{1,0:T(8,128)(2,1)}, f32[384,512]{1,0:T(8,128)}, f32[256,512]{1,0:T(8,128)}, f32[256,128]{1,0:T(8,128)}, f32[256,128]{1,0:T(8,1...) custom-call(bf16[384,512]{1,0:T(8,128)(2,1)} %get-tuple-element.21.refs_0_, f32[384,512]{1,0:T(8,128)} %get-tuple-element.22.refs_1_, ...), custom_call_target="tpu_custom_call" | custom-call | tf_op jit(solution)/shard_map/place_results/pallas_call | solution.py:804

commit v7 on v6

--- a/solution.py
+++ b/solution.py
@@ -201,6 +201,9 @@
 
         def add(self, h, a, b, s, *terms):
             j, rows = spot(h, a, b), self.part(h, s)
+            if len(terms) == 1:
+                self.buf[j, rows] += terms[0][...]
+                return
             total = self.buf[j, rows].astype(F32)
             for term in terms:
                 total = total + term[...].astype(F32)
@@ -248,7 +251,7 @@
 
         def add(self, k, i, rows, term):
             j = self.block(k, 1) + i
-            self.buf[j, rows] = (self.buf[j, rows].astype(F32) + term.astype(F32)).astype(BF16)
+            self.buf[j, rows] += term
 
         def swap(self, k):
             start(self.buf.at[pl.ds(self.block(k, 0), 2)], self.r_core.at[k], "core", self.t, self.t * 8 + k, along("core", 1))

time: 128 us -> 128 us (level)
  no operation moved by 1% of the time
where the time goes in v7:
time: 128 us
  Pallas kernels  126 us (98%)
  between operations  2.1 us (2%)
    pallas_call x1, Pallas kernels, shards(): pl.pallas_call(kernel, out_shape=results, in_specs=[anywhere, anywhere, a...  123 us
    pallas_call x1, Pallas kernels, shards(): pl.pallas_call(place_kernel, out_shape=tuple((jax.ShapeDtypeStruct(out.sh...  2.69 us

profile of v7, /device:TPU:1, one launch (start us, length us, event | category | flops | bytes accessed | tf_op | source)
XLA Modules:
  0.0 128.1 jit_solution(4864942585045319358)
XLA Ops:
  1.9 123.3 %attention_step.1 = (bf16[384,512]{1,0:T(8,128)(2,1)}, f32[384,512]{1,0:T(8,128)}, f32[256,512]{1,0:T(8,128)}, f32[256,128]{1,0:T(8,128)}, f32[256,128]{1,0:T(8,...) custom-call(bf16[384,4096]{1,0:T(8,128)(2,1)} %bitcast.8, bf16[384,4096]{1,0:T(8,128)(2,1)} %bitcast.9, ...), custom_call_target="tpu_custom_call" | custom-call | tf_op jit(solution)/shard_map/attention_step/pallas_call | solution.py:793
  125.2 2.7 %place_results.1 = (bf16[384,512]{1,0:T(8,128)(2,1)}, f32[384,512]{1,0:T(8,128)}, f32[256,512]{1,0:T(8,128)}, f32[256,128]{1,0:T(8,128)}, f32[256,128]{1,0:T(8,1...) custom-call(bf16[384,512]{1,0:T(8,128)(2,1)} %get-tuple-element.21.refs_0_, f32[384,512]{1,0:T(8,128)} %get-tuple-element.22.refs_1_, ...), custom_call_target="tpu_custom_call" | custom-call | tf_op jit(solution)/shard_map/place_results/pallas_call | solution.py:807
